TPU v7x, 512 devices: a whole 4x4x16 slice. The times are simulated.
512 devices in a mesh: expert: 16 (over z), tensor: 32 (over y, x, core).
Axes of the slice: x: 4, y: 4, z: 16, core: 2. Of those that a mesh axis runs over, the one named last changes fastest.
Arguments:
- tokens: bfloat16 [1024, 3072], P('expert', 'tensor'), may hold values from -6 to 6
- grad_out: bfloat16 [1024, 3072], P('expert', 'tensor'), may hold values from -3 to 3
- probs: bfloat16 [1024, 4], P('expert'), may hold values from 0.049804688 to 0.5
- routes: int32 [1024, 4], P('expert'), may hold values from 0 to 15, all different within a row; in each aligned block of 64 rows (0 to 63, 64 to 127, ...) at most 20 rows name the same one
- gate_weight: bfloat16 [16, 5376, 3072], P('expert', 'tensor'), may hold values from -0.109375 to 0.109375
- up_weight: bfloat16 [16, 5376, 3072], P('expert', 'tensor'), may hold values from -0.109375 to 0.109375
- down_weight: bfloat16 [16, 5376, 3072], P('expert', 'tensor'), may hold values from -0.078125 to 0.078125
Outputs:
- d_tokens: bfloat16 [1024, 3072], P('expert', 'tensor')
- d_probs: float32 [1024, 4], P('expert')
- d_down: bfloat16 [16, 5376, 3072], P('expert', 'tensor')
Inputs may be any that keep to these rules, and one draw needn't show every extreme that they name: Each token's 4 experts differ. Among the 64 tokens of one index of expert, no expert is named by more than 20 routes, a bound that some block reaches of them.
All inputs are finite; a program needn't handle non-finite values.
Results may differ from a plain program's by a relative error of at most 0.007.
Values may be sent and summed in bfloat16 or wider, within the bound.
No kernel may reach another device: no remote copies, remote signals or barrier semaphores. Data moves between devices by JAX's collectives and lax.ppermute only.
A program may use at most 128 MiB of HBM per device.

v0:
```python
import jax
import jax.numpy as jnp
from jax import lax
from jax.sharding import PartitionSpec as P

TOK_DEV = 64
SLOTS = 320


def per_device(tokens, grad_out, probs, routes, gate_weight, up_weight, down_weight):
    n_experts = lax.axis_size("expert")
    capacity = min(SLOTS // n_experts, TOK_DEV)
    slots = n_experts * capacity
    tok_rows = routes.shape[0]
    top_count = routes.shape[1]
    flat_routes = routes.reshape(-1)
    pair_count = flat_routes.shape[0]
    experts_iota = lax.broadcasted_iota(jnp.int32, (pair_count, n_experts), 1)
    onehot = (flat_routes[:, None] == experts_iota).astype(jnp.int32)
    before = jnp.cumsum(onehot, axis=0) - onehot
    position = jnp.sum(before * onehot, axis=1)
    pair_slot = flat_routes * capacity + position
    slot_iota = lax.broadcasted_iota(jnp.int32, (slots, pair_count), 0)
    placer = (pair_slot[None, :] == slot_iota).astype(jnp.float32)
    token_placer = placer.reshape(slots, tok_rows, top_count).sum(axis=2)
    placer_half = placer.astype(jnp.bfloat16)
    token_half = token_placer.astype(jnp.bfloat16)
    send_probs = (
        jnp.dot(placer_half, probs.reshape(-1), preferred_element_type=jnp.float32)
        .astype(jnp.bfloat16)
        .reshape(n_experts, capacity)
    )
    send_x = (
        jnp.dot(token_half, tokens, preferred_element_type=jnp.float32)
        .astype(jnp.bfloat16)
        .reshape(n_experts, capacity, -1)
    )
    send_dy = (
        jnp.dot(token_half, grad_out, preferred_element_type=jnp.float32)
        .astype(jnp.bfloat16)
        .reshape(n_experts, capacity, -1)
    )
    got_x, got_dy, got_probs = (
        lax.all_to_all(send_x, "expert", split_axis=0, concat_axis=0, tiled=True),
        lax.all_to_all(send_dy, "expert", split_axis=0, concat_axis=0, tiled=True),
        lax.all_to_all(send_probs, "expert", split_axis=0, concat_axis=0, tiled=True),
    )
    rows_x, rows_dy = (
        lax.all_gather(got_x, "tensor", axis=2, tiled=True),
        lax.all_gather(got_dy, "tensor", axis=2, tiled=True),
    )
    rows_x = rows_x.reshape(slots, -1)
    rows_dy = rows_dy.reshape(slots, -1)
    prob_rows = got_probs.reshape(slots).astype(jnp.float32)
    w_gate = gate_weight[0]
    w_up = up_weight[0]
    w_down = down_weight[0]
    contract_last = (((1,), (1,)), ((), ()))
    pre_gate = lax.dot_general(rows_x, w_gate, contract_last, preferred_element_type=jnp.float32)
    pre_up = lax.dot_general(rows_x, w_up, contract_last, preferred_element_type=jnp.float32)
    sigmoid_a = jax.nn.sigmoid(pre_gate)
    silu_a = pre_gate * sigmoid_a
    hidden = (silu_a * pre_up).astype(jnp.bfloat16)
    back_hidden = lax.dot_general(
        rows_dy, w_down, contract_last, preferred_element_type=jnp.float32
    )
    score_part = jnp.sum(hidden.astype(jnp.float32) * back_hidden, axis=1)
    scaled_hidden = (prob_rows[:, None] * hidden.astype(jnp.float32)).astype(jnp.bfloat16)
    down_grad = lax.dot_general(
        scaled_hidden, rows_dy, (((0,), (0,)), ((), ())), preferred_element_type=jnp.float32
    ).astype(jnp.bfloat16)
    hidden_grad = prob_rows[:, None] * back_hidden
    grad_gate = (hidden_grad * pre_up * sigmoid_a * (1.0 + pre_gate * (1.0 - sigmoid_a))).astype(
        jnp.bfloat16
    )
    grad_up = (hidden_grad * silu_a).astype(jnp.bfloat16)
    input_grad = jnp.dot(grad_gate, w_gate, preferred_element_type=jnp.float32) + jnp.dot(
        grad_up, w_up, preferred_element_type=jnp.float32
    )
    scores = lax.psum(score_part, "tensor")
    score_block = scores.reshape(n_experts, capacity)
    grad_block = input_grad.reshape(n_experts, capacity, -1)
    placer_back = token_placer.T
    shares = lax.psum_scatter(grad_block, "tensor", scatter_dimension=2, tiled=True)
    back_rows, back_scores = (
        lax.all_to_all(shares, "expert", split_axis=0, concat_axis=0, tiled=True),
        lax.all_to_all(score_block, "expert", split_axis=0, concat_axis=0, tiled=True),
    )
    token_grad = jnp.dot(placer_back, back_rows.reshape(slots, -1), precision=lax.Precision.HIGHEST)
    d_tokens = token_grad.astype(jnp.bfloat16)
    d_probs = jnp.dot(
        placer.T, back_scores.reshape(slots), precision=lax.Precision.HIGHEST
    ).reshape(tok_rows, top_count)
    return (d_tokens, d_probs, down_grad[None])


def solution(mesh):
    return jax.shard_map(
        per_device,
        mesh=mesh,
        in_specs=(
            P("expert", "tensor"),
            P("expert", "tensor"),
            P("expert", None),
            P("expert", None),
            P("expert", "tensor", None),
            P("expert", "tensor", None),
            P("expert", "tensor", None),
        ),
        out_specs=(P("expert", "tensor"), P("expert", None), P("expert", "tensor", None)),
        check_vma=False,
    )
```

profile of v0, /device:TPU:24, one launch (start us, length us, event | category | flops | bytes accessed | tf_op | source)
XLA Modules:
  0.0 401.5 jit_solution(11952784950082843953)
XLA Ops:
  7.2 0.8 copy.50
  9.4 0.7 multiply_add_fusion
  10.2 0.9 convolution_convert_fusion.1
  11.3 28.6 %all_to_all.34 = bf16[16,20,96]{2,1,0:T(8,128)(2,1)S(1)} all-to-all(bf16[16,20,96]{2,1,0:T(8,128)(2,1)S(1)} %reshape.107), channel_id=1, replica_groups=mesh['expert'=16,'tensor'=32] {'expert'}, dimensions={0} | all-to-all | bytes 122880 | tf_op jit(solution)/shard_map/all_to_all | solution.py:44
  39.9 1.1 copy.60
  41.0 0.9 convolution_convert_fusion.2
  42.1 16.5 %all_to_all.35 = bf16[16,20,96]{2,1,0:T(8,128)(2,1)S(1)} all-to-all(bf16[16,20,96]{2,1,0:T(8,128)(2,1)S(1)} %reshape.105), channel_id=1, replica_groups=mesh['expert'=16,'tensor'=32] {'expert'}, dimensions={0} | all-to-all | bytes 122880 | tf_op jit(solution)/shard_map/all_to_all | solution.py:45
  58.7 1.1 copy.57
  60.5 15.7 %all_to_all.36 = bf16[16,1,20]{2,1,0:T(2,128)(2,1)S(1)} all-to-all(bf16[16,1,20]{2,1,0:T(2,128)(2,1)S(1)} %all_to_all.28), channel_id=1, replica_groups=mesh['expert'=16,'tensor'=32] {'expert'}, dimensions={0} | all-to-all | bytes 1280 | tf_op jit(solution)/shard_map/all_to_all | solution.py:46
  76.2 35.4 %all-gather.5.cloned.1.call-done = bf16[16,20,3072]{1,0,2:T(8,128)(2,1)} async-done(((bf16[16,20,96]{1,0,2:T(8,128)(2,1)}), bf16[16,20,3072]{1,0,2:T(8,128)(2,1)}) %all-gather.5.cloned.1.call-update) | async-done | bytes 1966096 | tf_op jit(solution)/shard_map/all_gather | solution.py:49
  111.6 16.1 %reshape.119 = bf16[320,3072]{0,1:T(8,128)(2,1)S(1)} reshape(bf16[16,20,3072]{1,0,2:T(8,128)(2,1)} %all-gather.5.cloned.1.call-done) | data formatting | bytes 3932160 | tf_op jit(solution)/shard_map/reshape | solution.py:52
  127.7 1.4 fusion.3
  129.1 1.4 fusion.6
  130.5 62.1 %all-gather.3.cloned.1.call-done = bf16[16,20,3072]{1,0,2:T(8,128)(2,1)} async-done(((bf16[16,20,96]{1,0,2:T(8,128)(2,1)}), bf16[16,20,3072]{1,0,2:T(8,128)(2,1)}) %all-gather.3.cloned.1.call-update) | async-done | bytes 1966096 | tf_op jit(solution)/shard_map/all_gather | solution.py:50
  192.7 16.1 %reshape.118 = bf16[320,3072]{0,1:T(8,128)(2,1)S(1)} reshape(bf16[16,20,3072]{1,0,2:T(8,128)(2,1)} %all-gather.3.cloned.1.call-done) | data formatting | bytes 3932160 | tf_op jit(solution)/shard_map/reshape | solution.py:53
  208.8 2.7 fusion.13
  211.5 0.8 fusion.1
  212.7 2.7 convolution_add_fusion
  215.4 4.9 %reshape.109 = f32[16,20,3072]{2,1,0:T(8,128)} reshape(f32[320,3072]{1,0:T(8,128)} %convolution_add_fusion) | data formatting | bytes 7864320 | tf_op jit(solution)/shard_map/reshape | solution.py:82
  220.3 14.3 %copy.65 = f32[16,20,3072]{1,0,2:T(8,128)} copy(f32[16,20,3072]{2,1,0:T(8,128)} %reshape.109) | data formatting | bytes 7864320
  234.5 19.6 %reshape.121 = f32[3072,320]{1,0:T(8,128)} reshape(f32[3072,16,20]{2,1,0:T(8,128)} %bitcast.58) | data formatting | bytes 7864320
  254.2 56.0 %psum.7 = f32[16,1,20]{2,1,0:T(1,128)} all-reduce(f32[16,1,20]{2,1,0:T(1,128)S(1)} %all_to_all.26), channel_id=1, replica_groups=mesh['expert'=16,'tensor'=32] {'tensor'}, use_global_device_ids=true, to_apply=%region_6.7 | all-reduce | flops 320 | bytes 2560 | tf_op jit(solution)/shard_map/psum | solution.py:80
  310.3 12.3 %all-to-all-start.4 = ((f32[16,1,20]{2,1,0:T(1,128)}), f32[16,1,20]{2,1,0:T(1,128)S(1)}, u32[]{:S(2)}, u32[]{:S(2)}) async-start(f32[16,1,20]{2,1,0:T(1,128)} %psum.7), calls=%async_computation.4 | async-start | bytes 16384 | tf_op jit(solution)/shard_map/all_to_all | solution.py:87
  322.6 38.0 %reduce-scatter.4.cloned.1.call-done = f32[96,320]{1,0:T(8,128)} async-done(((f32[3072,320]{1,0:T(8,128)}), f32[96,320]{1,0:T(8,128)}) %reduce-scatter.4.cloned.1.call-update) | async-done | bytes 122896
  360.6 2.3 reshape.122
  362.9 2.2 copy.66
  365.1 12.3 %all-to-all-start.3 = ((f32[16,20,96]{2,1,0:T(8,128)}), f32[16,20,96]{2,1,0:T(8,128)}, u32[]{:S(2)}, u32[]{:S(2)}) async-start(f32[16,20,96]{2,1,0:T(8,128)} %copy.66), calls=%async_computation.3 | async-start | bytes 393216 | tf_op jit(solution)/shard_map/all_to_all | solution.py:86
  377.4 2.8 fusion
  381.5 1.1 fusion.11
  382.6 10.6 %all-to-all-done.3 = f32[16,20,96]{2,1,0:T(8,128)} async-done(((f32[16,20,96]{2,1,0:T(8,128)}), f32[16,20,96]{2,1,0:T(8,128)}, u32[]{:S(2)}, u32[]{:S(2)}) %all-to-all-start.3) | async-done | bytes 122912 | tf_op jit(solution)/shard_map/all_to_all | solution.py:86
  393.2 0.9 reshape.110
  394.1 0.9 convolution_convert_fusion.3
  (47 shorter events, 4.4 us)
Async XLA Ops:
  7.2 120.5 %copy-start = (bf16[1,168,3072]{2,1,0:T(8,128)(2,1)S(1)}, bf16[1,168,3072]{2,1,0:T(8,128)(2,1)}, u32[]{:S(2)}) copy-start(bf16[1,168,3072]{2,1,0:T(8,128)(2,1)} %param.11) | copy-start | bytes 3096580
  7.2 52.7 %copy-start.6 = (bf16[64,4]{0,1:T(4,128)(2,1)S(1)}, bf16[64,4]{0,1:T(4,128)(2,1)}, u32[]{:S(2)}) copy-start(bf16[64,4]{0,1:T(4,128)(2,1)} %param.9) | copy-start | bytes 1540
  7.2 104.4 %all-gather.5.cloned.1.call-start = ((), (), s32[]{:S(2)}) async-start(), calls=%async_computation.7 | async-start | bytes 12976128 | tf_op jit(solution)/shard_map/all_gather | solution.py:49
  41.0 151.7 %all-gather.3.cloned.1.call-start = ((), (), s32[]{:S(2)}) async-start(), calls=%async_computation.6 | async-start | bytes 12976128 | tf_op jit(solution)/shard_map/all_gather | solution.py:50
  59.9 300.7 %reduce-scatter.4.cloned.1.call-start = ((), (), s32[]{:S(2)}) async-start(), calls=%async_computation.8 | async-start | bytes 4866048
  127.7 1.4 copy-start.2
  208.7 2.8 copy-start.4
  208.7 2.8 copy-start.5
  211.5 1.2 copy-start.3
  310.3 54.8 %all-to-all-start.4 = ((f32[16,1,20]{2,1,0:T(1,128)}), f32[16,1,20]{2,1,0:T(1,128)S(1)}, u32[]{:S(2)}, u32[]{:S(2)}) async-start(f32[16,1,20]{2,1,0:T(1,128)} %psum.7), calls=%async_computation.4 | async-start | bytes 16384 | tf_op jit(solution)/shard_map/all_to_all | solution.py:87
  362.9 32.1 %copy-start.1 = (bf16[1,168,3072]{2,1,0:T(8,128)(2,1)S(1)}, bf16[1,168,3072]{2,1,0:T(8,128)(2,1)}, u32[]{:S(2)}) copy-start(bf16[1,168,3072]{2,1,0:T(8,128)(2,1)} %param.11) | copy-start | bytes 3096580
  365.1 28.1 %all-to-all-start.3 = ((f32[16,20,96]{2,1,0:T(8,128)}), f32[16,20,96]{2,1,0:T(8,128)}, u32[]{:S(2)}, u32[]{:S(2)}) async-start(f32[16,20,96]{2,1,0:T(8,128)} %copy.66), calls=%async_computation.3 | async-start | bytes 393216 | tf_op jit(solution)/shard_map/all_to_all | solution.py:86
Sparse Core Ops, SparseCore 0:
  41.1 70.4 all-gather.4
  114.7 77.8 all-gather.2
  254.3 106.2 reduce-scatter.3
where the time goes:
time: 403 us; the launch traced here: 402 us
  waiting for transfers between devices  146 us (36%)
  blocking collectives  117 us (29%)
  local copies, waits for them, and re-layouts  81.8 us (20%)
  starting transfers between devices  24.7 us (6%)
  matrix products  15.8 us (4%)
  between operations  14 us (3%)
    all_gather x1, waiting for transfers between devices, per_device(): lax.all_gather(got_dy, 'tensor', axis=2, tiled=True)  62.1 us
    psum x1, blocking collectives, per_device(): scores = lax.psum(score_part, 'tensor')  56 us
    unnamed x20, local copies, waits for them, and re-layouts  39.8 us
    unnamed x4, waiting for transfers between devices  38.1 us
    all_gather x1, waiting for transfers between devices, per_device(): lax.all_gather(got_x, 'tensor', axis=2, tiled=True)  35.4 us
    all_to_all x1, blocking collectives, per_device(): lax.all_to_all(send_x, 'expert', split_axis=0, concat_axis=0, tiled=True)  28.6 us
    all_to_all x1, blocking collectives, per_device(): lax.all_to_all(send_dy, 'expert', split_axis=0, concat_axis=0, tiled=True)  16.5 us
    reshape x1, local copies, waits for them, and re-layouts, per_device(): rows_x = rows_x.reshape(slots, -1)  16.1 us
  transfers between devices with their start and end apart: 5, of which 4 were waited for; matrix products, arithmetic and copies ran while one was open for 8% of the time, Pallas kernels for 0%

commit v1 on v0

v1 whole, which is shorter than its diff:
```python
import jax
import jax.numpy as jnp
from jax import lax
from jax.experimental import pallas as pl
from jax.experimental.pallas import tpu as pltpu
from jax.sharding import PartitionSpec as P

F32 = jnp.float32
BF16 = jnp.bfloat16
I32 = jnp.int32

EXPERTS = 16
CHIPS = 16
CAP = 20
SLOTS = EXPERTS * CAP
WIDE = 384
TOK = 64
TOP = 4
FEAT = 96
HID = 168
D = 3072
BLOCK = 32


def iota(shape, dim):
    return lax.broadcasted_iota(I32, shape, dim)


def flag(condition):
    return jnp.where(condition, 1.0, 0.0).astype(F32)


def hot(condition):
    return flag(condition).astype(BF16)


def dot(a, b):
    return jnp.dot(a, b, preferred_element_type=F32)


def dot_first(a, b):
    return lax.dot_general(a, b, (((0,), (0,)), ((), ())), preferred_element_type=F32)


def dot_last(a, b):
    return lax.dot_general(a, b, (((1,), (1,)), ((), ())), preferred_element_type=F32)


def expert_of(slot):
    return lax.shift_right_logical(slot * 3277, 16)


def params(mib, **kw):
    return pltpu.CompilerParams(vmem_limit_bytes=mib * 1024 * 1024, **kw)


def cost(flops):
    return pl.CostEstimate(flops=int(flops), bytes_accessed=4 << 20, transcendentals=0)


def pack_kernel(routes_hbm, probs_hbm, x_hbm, dy_hbm, out_ref, row_ref, routes_ref, probs_ref, x_ref, dy_ref, sems):
    pairs = ((routes_hbm, routes_ref), (probs_hbm, probs_ref), (x_hbm, x_ref), (dy_hbm, dy_ref))
    loads = [pltpu.make_async_copy(src, dst, sems.at[i]) for i, (src, dst) in enumerate(pairs)]
    for load in loads:
        load.start()
    for load in loads:
        load.wait()
    routes = routes_ref[...]
    probs = probs_ref[...].astype(F32)
    experts = iota((EXPERTS, TOK), 0)
    hits = [routes[k : k + 1, :] == experts for k in range(TOP)]
    member = sum(flag(h) for h in hits)
    weight = sum(jnp.where(hits[k], probs[k : k + 1, :], 0.0) for k in range(TOP))
    upper = hot(iota((TOK, TOK), 0) < iota((TOK, TOK), 1))
    count = dot(member.astype(BF16), upper)
    place = jnp.where(member > 0.5, count, -1.0)
    target = count + (experts * BLOCK).astype(F32)
    rows_of = [jnp.sum(jnp.where(hits[k], target, 0.0), axis=0, keepdims=True) for k in range(TOP)]
    kth = iota((8, TOK), 0)
    row_ref[...] = sum(jnp.where(kth == k, rows_of[k], 0.0) for k in range(TOP)).astype(I32)

    rows = EXPERTS * BLOCK
    expand = hot(lax.shift_right_logical(iota((rows, EXPERTS), 0), 5) == iota((rows, EXPERTS), 1))
    place_rows = dot(expand, place.astype(BF16))
    weight_rows = dot(expand, weight.astype(BF16))
    s_int = iota((rows, TOK), 0) & (BLOCK - 1)
    s = s_int.astype(F32)
    tail = (s_int >= CAP) & (s_int < 30)
    main = flag((place_rows == s) & (s_int < CAP))
    left = hot((place_rows == s - 20.0) & tail)
    right = hot((place_rows == s - 10.0) & tail)

    x = x_ref[...]
    dy = dy_ref[...]
    f = iota((FEAT, 128), 0)
    lane = iota((FEAT, 128), 1)
    b_main = dot(x, hot(lane == f)) + dot(dy, hot((lane == f + 96) & (f < 32)))
    b_left = dot(dy, hot((lane == f - 32) & (f >= 32)))
    b_right = dot(dy, hot((lane == f + 32) & (f >= 32)))

    prob_col = jnp.sum(main * weight_rows, axis=1, keepdims=True)
    s_lane = iota((rows, 128), 0) & (BLOCK - 1)
    prob_wide = jnp.where(s_lane == iota((rows, 128), 1), prob_col, 0.0).astype(BF16)
    gather = hot(lax.shift_right_logical(iota((EXPERTS, rows), 1), 5) == iota((EXPERTS, rows), 0))
    prob_block = dot(gather, prob_wide).astype(BF16)
    at_30 = hot(iota((rows, EXPERTS), 0) == iota((rows, EXPERTS), 1) * BLOCK + 30)

    out = (
        dot(main.astype(BF16), b_main.astype(BF16))
        + dot(left, b_left.astype(BF16))
        + dot(right, b_right.astype(BF16))
        + dot(at_30, prob_block)
    )
    out_ref[...] = out.astype(BF16).reshape(EXPERTS, BLOCK, 128)


def spread_kernel(got_ref, out_ref, prob_ref):
    rows = EXPERTS * BLOCK
    got = got_ref[...].reshape(rows, 128)
    n = iota((1, WIDE), 1)
    e_x = expert_of(n)
    s_x = n - e_x * CAP
    to_x = jnp.where(n < SLOTS, e_x * BLOCK + s_x, -1)
    slot = jnp.where(n < 128, n + 192, n - 128)
    e_d = expert_of(slot)
    s_d = slot - e_d * CAP
    live = n >= 64
    to_d = jnp.where(live, e_d * BLOCK + s_d, -1)
    to_left = jnp.where(live & (s_d < 10), e_d * BLOCK + 20 + s_d, -1)
    to_right = jnp.where(live & (s_d >= 10), e_d * BLOCK + 10 + s_d, -1)
    r = iota((rows, WIDE), 0)
    part_x = dot_first(got, hot(r == to_x))
    part_d = dot_first(got, hot(r == to_d))
    part_l = dot_first(got, hot(r == to_left))
    part_r = dot_first(got, hot(r == to_right))
    x_t = part_x[0:FEAT]
    d_t = jnp.concatenate([part_d[96:128], part_l[0:64] + part_r[64:128]], axis=0)
    first = x_t[:, 0:256].astype(BF16)
    middle = (x_t[:, 256:384] + d_t[:, 0:128]).astype(BF16)
    last = d_t[:, 128:384].astype(BF16)
    for j in range(CHIPS):
        out_ref[j, :, 0:256] = first
        out_ref[j, :, 256:384] = middle
        out_ref[j, :, 384:640] = last

    pick = hot(iota((EXPERTS, rows), 1) == iota((EXPERTS, rows), 0) * BLOCK + 30)
    per_expert = dot(pick, got).astype(BF16)
    wide = dot(per_expert, hot(iota((128, WIDE), 0) == s_x))
    probs = jnp.sum(jnp.where(iota((EXPERTS, WIDE), 0) == e_x, wide, 0.0), axis=0, keepdims=True)
    prob_ref[...] = jnp.broadcast_to(probs, (8, WIDE))


def score_rows(scores):
    row = iota((16, 128), 0)
    return (
        jnp.where(row == 0, scores[:, 0:128], 0.0)
        + jnp.where(row == 1, scores[:, 128:256], 0.0)
        + jnp.where(row == 2, scores[:, 256:384], 0.0)
    )


def split_rows(scores):
    high = scores.astype(BF16).astype(F32)
    low = (scores - high).astype(BF16).astype(F32)
    return (high + pltpu.roll(low, 3, 0)).astype(BF16)


def squeeze(piece):
    last = piece[:, 256:384]
    lane = iota((48, 128), 1)
    both = jnp.where(lane < 64, last[0:48], pltpu.roll(last[48:96], 64, 1))
    return piece[:, 0:128], piece[:, 128:256], both


def this_core():
    return lax.rem(lax.axis_index("tensor"), 2)


def turn_kernel(own_ref, gate_ref, up_ref, rows_ref, gate_t_ref, up_t_ref):
    core = this_core()
    first = core == 0
    for j in range(CHIPS):
        rows_ref[j, core] = own_ref[j]
    for weight_ref, turned_ref in ((gate_ref, gate_t_ref), (up_ref, up_t_ref)):
        for i in range(CHIPS // 2):
            turned = weight_ref[0, :, pl.ds(i * 384, 384)].T
            for half in range(2):
                even = turned[192 * half : 192 * half + 96]
                odd = turned[192 * half + 96 : 192 * half + 192]
                turned_ref[0, 2 * i + half] = jnp.where(first, odd, even)
                turned_ref[1, 2 * i + half] = jnp.where(first, even, odd)


def input_grads(turned, gate_t_ref, up_t_ref, grad_gate, grad_up, out_ref):
    for i in range(0, CHIPS, 4):
        part = pl.ds(i, 4)
        sums = dot(gate_t_ref[turned, part].reshape(384, HID), grad_gate)
        sums = sums + dot(up_t_ref[turned, part].reshape(384, HID), grad_up)
        for j in range(4):
            a, b, c = squeeze(sums[96 * j : 96 * j + 96])
            out_ref[i + j, 0:96] = a.astype(out_ref.dtype)
            out_ref[i + j, 96:192] = b.astype(out_ref.dtype)
            out_ref[i + j, 192:240] = c.astype(out_ref.dtype)


def middle_kernel(
    rows_in_ref,
    other_ref,
    gate_ref,
    up_ref,
    down_ref,
    prob_ref,
    gate_t_ref,
    up_t_ref,
    rows_ref,
    send_ref,
    score_ref,
    hid_ref,
):
    del rows_in_ref
    core = this_core()
    for j in range(CHIPS):
        rows_ref[j, 1 - core] = other_ref[j]
    rows = rows_ref[...].reshape(D, 640)
    x_t = rows[:, 0:384]
    dy_t = rows[:, 256:640]
    pre_gate = dot(gate_ref[0], x_t)
    pre_up = dot(up_ref[0], x_t)
    raw = dot(down_ref[0], dy_t)
    back = jnp.concatenate([raw[:, 128:384], pltpu.roll(raw[:, 0:128], 64, 1)], axis=1)
    live = iota((1, WIDE), 1) < SLOTS
    back = jnp.where(live, back, 0.0)
    probs = prob_ref[0:1, :]
    sig = jax.nn.sigmoid(pre_gate)
    silu = pre_gate * sig
    hidden = (silu * pre_up).astype(BF16).astype(F32)
    scores = score_rows(jnp.sum(hidden * back, axis=0, keepdims=True))
    scaled = jnp.where(live, probs * hidden, 0.0)
    back_p = probs * back
    grad_gate = jnp.where(live, back_p * pre_up * sig * (1.0 + pre_gate * (1.0 - sig)), 0.0).astype(BF16)
    grad_up = (back_p * silu).astype(BF16)
    input_grads(0, gate_t_ref, up_t_ref, grad_gate, grad_up, send_ref)
    parts = split_rows(scores)
    for j in range(CHIPS):
        send_ref[j, 240:256] = parts
    score_ref[...] = scores
    scaled = jnp.concatenate([pltpu.roll(scaled[:, 256:384], 64, 1), scaled[:, 0:256]], axis=1)
    hid_ref[0] = scaled.astype(BF16)
    hid_ref[1] = grad_gate
    hid_ref[2] = grad_up


def rest_kernel(rows_ref, hid_ref, gate_t_ref, up_t_ref, keep_ref, d_down_ref):
    d_down_ref[0] = dot_last(hid_ref[0], rows_ref[...].reshape(D, 640)[:, 256:640]).astype(BF16)
    input_grads(1, gate_t_ref, up_t_ref, hid_ref[1], hid_ref[2], keep_ref)


def join_kernel(keep_ref, score_ref, got_ref, out_ref):
    got = got_ref[0, 240:256].astype(F32)
    row = iota((16, 128), 0)
    total = score_ref[...] + got + pltpu.roll(got, 13, 0)
    parts = split_rows(jnp.where(row < 3, total, 0.0))
    for j in range(CHIPS):
        out_ref[j, 0:240] = (keep_ref[j, 0:240] + got_ref[j, 0:240].astype(F32)).astype(BF16)
        out_ref[j, 240:256] = parts


def fold_kernel(got_ref, out_ref):
    total = got_ref[0].astype(F32)
    for j in range(1, CHIPS):
        total = total + got_ref[j].astype(F32)
    both = total[192:240]
    lane = iota((48, 128), 1)
    last = jnp.concatenate(
        [jnp.where(lane < 64, both, 0.0), jnp.where(lane < 64, pltpu.roll(both, 64, 1), 0.0)], axis=0
    )
    grads = jnp.concatenate([total[0:96], total[96:192], last], axis=1)
    tail = total[240:256]
    score = tail + pltpu.roll(tail, 13, 0)
    wide = jnp.concatenate([score[0:1], score[1:2], score[2:3]], axis=1)
    high = wide.astype(BF16).astype(F32)
    low = wide - high
    row = iota((32, WIDE), 0)
    extra = jnp.where(row == 0, high, 0.0) + jnp.where(row == 1, low, 0.0)
    table = jnp.concatenate([grads, extra], axis=0).astype(BF16)
    n = iota((1, WIDE), 1)
    e = expert_of(n)
    to = jnp.where(n < SLOTS, e * BLOCK + (n - e * CAP), -1)
    pick = hot(iota((EXPERTS * BLOCK, WIDE), 0) == to)
    out_ref[...] = dot_last(pick, table).astype(BF16).reshape(EXPERTS, BLOCK, 128)


def combine_kernel(got_ref, row_ref, d_tokens_ref, d_probs_ref):
    rows = EXPERTS * BLOCK
    got = got_ref[...].reshape(rows, 128)
    r = iota((rows, TOK), 0)
    picks = [flag(r == row_ref[k : k + 1, :]) for k in range(TOP)]
    d_tokens_ref[...] = dot_first(sum(picks).astype(BF16), got)[:, 0:FEAT].astype(BF16)
    lane = iota((rows, 128), 1)
    score = jnp.where((lane == 96) | (lane == 97), got.astype(F32), 0.0)
    score = jnp.sum(score, axis=1, keepdims=True)
    for k in range(TOP):
        d_probs_ref[k : k + 1, :] = jnp.sum(picks[k] * score, axis=0, keepdims=True)


def struct(*shape, dtype):
    return jax.ShapeDtypeStruct(shape, dtype)


SAME_CORE = [[2 * j + core for j in range(CHIPS)] for core in range(2)]
OTHER_CORE = [(i, i ^ 1) for i in range(2 * CHIPS)]


def per_device(tokens, grad_out, probs, routes, gate_weight, up_weight, down_weight):
    packed, row_of = pl.pallas_call(
        pack_kernel,
        out_shape=(pltpu.VMEM((EXPERTS, BLOCK, 128), BF16), pltpu.VMEM((8, TOK), I32)),
        in_specs=[pl.BlockSpec(memory_space=pltpu.HBM)] * 4,
        scratch_shapes=[
            pltpu.VMEM((TOP, TOK), I32),
            pltpu.VMEM((TOP, TOK), BF16),
            pltpu.VMEM((TOK, FEAT), BF16),
            pltpu.VMEM((TOK, FEAT), BF16),
            pltpu.SemaphoreType.DMA((4,)),
        ],
        compiler_params=params(60),
        name="pack",
    )(routes.T, probs.T, tokens, grad_out)
    got = lax.all_to_all(packed, "expert", 0, 0, tiled=True)
    copies, prob_rows = pl.pallas_call(
        spread_kernel,
        out_shape=(struct(CHIPS, FEAT, 640, dtype=BF16), struct(8, WIDE, dtype=F32)),
        compiler_params=params(16),
        name="spread",
    )(got)
    own = lax.all_to_all(copies, "tensor", 0, 0, tiled=True, axis_index_groups=SAME_CORE)
    other = lax.ppermute(own, "tensor", OTHER_CORE)
    rows, gate_t, up_t = pl.pallas_call(
        turn_kernel,
        out_shape=(
            struct(CHIPS, 2, FEAT, 640, dtype=BF16),
            struct(2, CHIPS, FEAT, HID, dtype=BF16),
            struct(2, CHIPS, FEAT, HID, dtype=BF16),
        ),
        compiler_params=params(20),
        cost_estimate=cost(8e9),
        name="turn",
    )(own, gate_weight, up_weight)
    rows, send, score, hid = pl.pallas_call(
        middle_kernel,
        out_shape=(
            struct(CHIPS, 2, FEAT, 640, dtype=BF16),
            struct(CHIPS, 256, 128, dtype=BF16),
            struct(16, 128, dtype=F32),
            struct(3, HID, WIDE, dtype=BF16),
        ),
        input_output_aliases={0: 0},
        compiler_params=params(24),
        cost_estimate=cost(4e9),
        name="middle",
    )(rows, other, gate_weight, up_weight, down_weight, prob_rows, gate_t, up_t)
    partner = lax.ppermute(send, "tensor", OTHER_CORE)
    keep, d_down = pl.pallas_call(
        rest_kernel,
        out_shape=(struct(CHIPS, 240, 128, dtype=F32), struct(1, HID, D, dtype=BF16)),
        compiler_params=params(20),
        cost_estimate=cost(4e9),
        name="rest",
    )(rows, hid, gate_t, up_t)
    joined = pl.pallas_call(
        join_kernel,
        out_shape=struct(CHIPS, 256, 128, dtype=BF16),
        compiler_params=params(16),
        name="join",
    )(keep, score, partner)
    shares = lax.all_to_all(joined, "tensor", 0, 0, tiled=True, axis_index_groups=SAME_CORE)
    folded = pl.pallas_call(
        fold_kernel,
        out_shape=struct(EXPERTS, BLOCK, 128, dtype=BF16),
        compiler_params=params(16),
        name="fold",
    )(shares)
    back = lax.all_to_all(folded, "expert", 0, 0, tiled=True)
    d_tokens, d_probs = pl.pallas_call(
        combine_kernel,
        out_shape=(struct(TOK, FEAT, dtype=BF16), struct(TOP, TOK, dtype=F32)),
        compiler_params=params(16),
        name="combine",
    )(back, row_of)
    return d_tokens, d_probs.T, d_down


def solution(mesh):
    return jax.shard_map(
        per_device,
        mesh=mesh,
        in_specs=(
            P("expert", "tensor"),
            P("expert", "tensor"),
            P("expert", None),
            P("expert", None),
            P("expert", "tensor", None),
            P("expert", "tensor", None),
            P("expert", "tensor", None),
        ),
        out_specs=(P("expert", "tensor"), P("expert", None), P("expert", "tensor", None)),
        check_vma=False,
    )
```

time: 403 us -> 119 us (0.30)
  waiting for transfers between devices: 146 us -> 2.93 us
  local copies, waits for them, and re-layouts: 81.8 us -> 0.02 us
  starting transfers between devices: 24.7 us -> 4.07 us
  blocking collectives: 117 us -> 99.2 us
  matrix products: 15.8 us -> 0 us
  between operations: 14 us -> 0.72 us
  Pallas kernels: 0 us -> 10.5 us
    all_gather x2 -> x0, waiting for transfers between devices: 97.5 us -> none  [the longest x1 62.1 us: per_device(): lax.all_gather(got_dy, 'tensor', axis=2, tiled=True)]
    psum x1 -> x0, blocking collectives: 56 us -> none  [per_device(): scores = lax.psum(score_part, 'tensor')]
    unnamed x20 -> x6, local copies, waits for them, and re-layouts: 39.8 us -> 0.02 us
    all_to_all x3 -> x4, blocking collectives: 60.8 us -> 99.2 us  [the longest x1 29.7 us: per_device(): got = lax.all_to_all(packed, 'expert', 0, 0, tiled=True)]
    reshape x8 -> x0, local copies, waits for them, and re-layouts: 38.2 us -> none  [the longest x1 16.1 us: per_device(): rows_x = rows_x.reshape(slots, -1)]
    unnamed x4 -> x0, waiting for transfers between devices: 38.1 us -> none
    all_to_all x2 -> x0, starting transfers between devices: 24.6 us -> none  [the longest x1 12.3 us: per_device(): lax.all_to_all(shares, 'expert', split_axis=0, concat_axis=0, tiled=True)]
    dot_general x11 -> x0, matrix products: 15.8 us -> none  [the longest x1 2.81 us: per_device(): lax.dot_general(scaled_hidden, rows_dy, (((0,), (0,)), ((), ())), preferr...]
  transfers between devices with their start and end apart: 5 -> 2, of which waited for: 4 -> 1; matrix products, arithmetic and copies ran while one was open for 8% -> 0% of each run, Pallas kernels for 0% -> 3%
where the time goes in v1:
time: 119 us; the launch traced here: 117 us
  blocking collectives  99.2 us (83%)
  Pallas kernels  10.5 us (9%)
  starting transfers between devices  4.07 us (3%)
  waiting for transfers between devices  2.93 us (2%)
    all_to_all x1, blocking collectives, per_device(): got = lax.all_to_all(packed, 'expert', 0, 0, tiled=True)  29.7 us
    all_to_all x1, blocking collectives, per_device(): lax.all_to_all(copies, 'tensor', 0, 0, tiled=True, axis_index_groups=SAME...  28.9 us
    all_to_all x1, blocking collectives, per_device(): lax.all_to_all(joined, 'tensor', 0, 0, tiled=True, axis_index_groups=SAME...  20.6 us
    all_to_all x1, blocking collectives, per_device(): back = lax.all_to_all(folded, 'expert', 0, 0, tiled=True)  20 us
    pallas_call x1, Pallas kernels, per_device(): pl.pallas_call(middle_kernel, out_shape=(struct(CHIPS, 2, FEAT, 640, dtyp...  3.28 us
    ppermute x1, waiting for transfers between devices, per_device(): other = lax.ppermute(own, 'tensor', OTHER_CORE)  2.93 us
    pallas_call x1, Pallas kernels, per_device(): pl.pallas_call(rest_kernel, out_shape=(struct(CHIPS, 240, 128, dtype=F32)...  2.6 us
  transfers between devices with their start and end apart: 2, of which 1 were waited for; matrix products, arithmetic and copies ran while one was open for 0% of the time, Pallas kernels for 3%

profile of v1, /device:TPU:24, one launch (start us, length us, event | category | flops | bytes accessed | tf_op | source)
XLA Modules:
  0.0 117.5 jit_solution(7505043256289713264)
XLA Ops:
  0.6 1.6 %pack.1 = (bf16[16,32,128]{2,1,0:T(8,128)(2,1)S(1)}, s32[8,64]{1,0:T(8,128)S(1)}) custom-call(s32[4,64]{1,0:T(4,128)} %bitcast.3, bf16[4,64]{1,0:T(4,128)(2,1)} %bitcast.4, bf16[64,96]{1,0:T(8,128)(2,1)} %x_hbm.1, bf16[64,96]{1,0:T(8,128)(2,1)} %dy_hbm.1), custom_call_target="tpu_custom_call" | custom-call | tf_op jit(solution)/shard_map/pack/pallas_call | solution.py:315
  2.2 29.7 %all_to_all.20.got_ref = bf16[16,32,128]{2,1,0:T(8,128)(2,1)S(1)} all-to-all(bf16[16,32,128]{2,1,0:T(8,128)(2,1)S(1)} %get-tuple-element.18), channel_id=1, replica_groups=mesh['expert'=16,'tensor'=32] {'expert'}, dimensions={0} | all-to-all | bytes 262144 | tf_op jit(solution)/shard_map/all_to_all | solution.py:329
  31.9 0.6 spread.1
  32.5 0.0 copy-start
  32.6 0.0 copy-start.1
  32.6 28.9 %all_to_all.21.own_ref = bf16[16,96,640]{2,1,0:T(8,128)(2,1)S(1)} all-to-all(bf16[16,96,640]{2,1,0:T(8,128)(2,1)S(1)} %get-tuple-element.19), channel_id=1, replica_groups={{0,2,4,6,8,10,12,14,16,18,20,22,24,26,28,30},{1,3,5,7,9,11,13,15,17,19,..., dimensions={0} | all-to-all | bytes 3932160 | tf_op jit(solution)/shard_map/all_to_all | solution.py:336
  61.5 0.0 copy-start.2
  61.5 2.0 %collective-permute-start = (bf16[16,96,640]{2,1,0:T(8,128)(2,1)S(1)}, bf16[16,96,640]{2,1,0:T(8,128)(2,1)S(1)}, u32[]{:S(2)}, u32[]{:S(2)}) collective-permute-start(bf16[16,96,640]{2,1,0:T(8,128)(2,1)S(1)} %all_to_all.21.own_ref), channel_id=1, source_target_pairs={{0,1},{1,0},{2,3},{3,2},{4,5},{5,4},{6,7},{7,6},{8,9},{9,8},{10,11... | collective-permute-start | bytes 5898248 | tf_op jit(solution)/shard_map/ppermute | solution.py:337
  63.5 0.0 copy-done
  63.5 0.0 copy-done.1
  63.5 1.0 turn.1
  64.5 2.9 %collective-permute-done.other_ref = bf16[16,96,640]{2,1,0:T(8,128)(2,1)S(1)} collective-permute-done((bf16[16,96,640]{2,1,0:T(8,128)(2,1)S(1)}, bf16[16,96,640]{2,1,0:T(8,128)(2,1)S(1)}, u32[]{:S(2)}, u32[]{:S(2)}) %collective-permute-start) | collective-permute-done | bytes 1966112 | tf_op jit(solution)/shard_map/ppermute | solution.py:337
  67.5 0.0 copy-done.2
  67.5 3.3 %middle.1 = (bf16[16,2,96,640]{3,2,1,0:T(8,128)(2,1)S(1)}, bf16[16,256,128]{2,1,0:T(8,128)(2,1)S(1)}, f32[16,128]{1,0:T(8,128)S(1)}, bf16[3,168,384]{2,1,0:T(8,128)(2,1)S(1)}) custom-call(bf16[16,2,96,640]{3,2,1,0:T(8,128)(2,1)S(1)} %get-tuple-element.20.rows_in_ref, ...), custom_call_target="tpu_custom_call", output_to_operand_aliasing={{0}: (0, {})} | custom-call | flops 4000000000 | bytes 4194304 | tf_op jit(solution)/shard_map/middle/pallas_call | solution.py:349
  70.7 2.0 %collective-permute-start.1 = (bf16[16,256,128]{2,1,0:T(8,128)(2,1)S(1)}, bf16[16,256,128]{2,1,0:T(8,128)(2,1)S(1)}, u32[]{:S(2)}, u32[]{:S(2)}) collective-permute-start(bf16[16,256,128]{2,1,0:T(8,128)(2,1)S(1)} %get-tuple-element.28), channel_id=1, source_target_pairs={{0,1},{1,0},{2,3},{3,2},{4,5},{5,4},{6,7},{7,6},{8,9},{9,8},{10,11... | collective-permute-start | bytes 3145736 | tf_op jit(solution)/shard_map/ppermute | solution.py:362
  72.8 2.6 %rest.1 = (f32[16,240,128]{2,1,0:T(8,128)S(1)}, bf16[1,168,3072]{2,1,0:T(8,128)(2,1)}) custom-call(bf16[16,2,96,640]{3,2,1,0:T(8,128)(2,1)S(1)} %get-tuple-element.24.rows_ref, bf16[3,168,384]{2,1,0:T(8,128)(2,1)S(1)} %get-tuple-element.25.hid_ref, bf16[2,16,96,168]{3,2,1,0:T(8,128)(2,1)S(1)} %get-tuple-element.22.gate_t_ref, ...), custom_call_target="tpu_custom_call" | custom-call | flops 4000000000 | bytes 4194304 | tf_op jit(solution)/shard_map/rest/pallas_call | solution.py:363
  75.4 0.0 collective-permute-done.1.got_ref
  75.4 0.2 join.1
  75.6 20.6 %all_to_all.22.got_ref = bf16[16,256,128]{2,1,0:T(8,128)(2,1)S(1)} all-to-all(bf16[16,256,128]{2,1,0:T(8,128)(2,1)S(1)} %join.1), channel_id=1, replica_groups={{0,2,4,6,8,10,12,14,16,18,20,22,24,26,28,30},{1,3,5,7,9,11,13,15,17,19,..., dimensions={0} | all-to-all | bytes 2097152 | tf_op jit(solution)/shard_map/all_to_all | solution.py:376
  96.2 0.4 fold.1
  96.6 20.0 %all_to_all.23.got_ref = bf16[16,32,128]{2,1,0:T(8,128)(2,1)S(1)} all-to-all(bf16[16,32,128]{2,1,0:T(8,128)(2,1)S(1)} %fold.1), channel_id=1, replica_groups=mesh['expert'=16,'tensor'=32] {'expert'}, dimensions={0} | all-to-all | bytes 262144 | tf_op jit(solution)/shard_map/all_to_all | solution.py:383
  116.6 0.9 combine.1
Async XLA Ops:
  32.5 31.0 %copy-start = (bf16[1,168,3072]{2,1,0:T(8,128)(2,1)S(1)}, bf16[1,168,3072]{2,1,0:T(8,128)(2,1)}, u32[]{:S(2)}) copy-start(bf16[1,168,3072]{2,1,0:T(8,128)(2,1)} %gate_ref.3) | copy-start | bytes 3096580
  32.6 31.0 %copy-start.1 = (bf16[1,168,3072]{2,1,0:T(8,128)(2,1)S(1)}, bf16[1,168,3072]{2,1,0:T(8,128)(2,1)}, u32[]{:S(2)}) copy-start(bf16[1,168,3072]{2,1,0:T(8,128)(2,1)} %up_ref.3) | copy-start | bytes 3096580
  61.5 6.0 %copy-start.2 = (bf16[1,168,3072]{2,1,0:T(8,128)(2,1)S(1)}, bf16[1,168,3072]{2,1,0:T(8,128)(2,1)}, u32[]{:S(2)}) copy-start(bf16[1,168,3072]{2,1,0:T(8,128)(2,1)} %down_ref.1) | copy-start | bytes 3096580
  61.5 6.0 %collective-permute-start = (bf16[16,96,640]{2,1,0:T(8,128)(2,1)S(1)}, bf16[16,96,640]{2,1,0:T(8,128)(2,1)S(1)}, u32[]{:S(2)}, u32[]{:S(2)}) collective-permute-start(bf16[16,96,640]{2,1,0:T(8,128)(2,1)S(1)} %all_to_all.21.own_ref), channel_id=1, source_target_pairs={{0,1},{1,0},{2,3},{3,2},{4,5},{5,4},{6,7},{7,6},{8,9},{9,8},{10,11... | collective-permute-start | bytes 5898248 | tf_op jit(solution)/shard_map/ppermute | solution.py:337
  70.7 4.6 %collective-permute-start.1 = (bf16[16,256,128]{2,1,0:T(8,128)(2,1)S(1)}, bf16[16,256,128]{2,1,0:T(8,128)(2,1)S(1)}, u32[]{:S(2)}, u32[]{:S(2)}) collective-permute-start(bf16[16,256,128]{2,1,0:T(8,128)(2,1)S(1)} %get-tuple-element.28), channel_id=1, source_target_pairs={{0,1},{1,0},{2,3},{3,2},{4,5},{5,4},{6,7},{7,6},{8,9},{9,8},{10,11... | collective-permute-start | bytes 3145736 | tf_op jit(solution)/shard_map/ppermute | solution.py:362

commit v2 on v1

--- a/solution.py
+++ b/solution.py
@@ -11,6 +11,7 @@
 
 EXPERTS = 16
 CHIPS = 16
+SIDE = 4
 CAP = 20
 SLOTS = EXPERTS * CAP
 WIDE = 384
@@ -138,7 +139,7 @@
     first = x_t[:, 0:256].astype(BF16)
     middle = (x_t[:, 256:384] + d_t[:, 0:128]).astype(BF16)
     last = d_t[:, 128:384].astype(BF16)
-    for j in range(CHIPS):
+    for j in range(SIDE):
         out_ref[j, :, 0:256] = first
         out_ref[j, :, 256:384] = middle
         out_ref[j, :, 384:640] = last
@@ -176,19 +177,41 @@
     return lax.rem(lax.axis_index("tensor"), 2)
 
 
-def turn_kernel(own_ref, gate_ref, up_ref, rows_ref, gate_t_ref, up_t_ref):
+def relay_kernel(got_ref, out_ref):
+    for j in range(SIDE):
+        out_ref[j] = got_ref[...]
+
+
+def chip_of(i, core):
+    return jnp.where(core == 0, i, (i % SIDE) * SIDE + i // SIDE)
+
+
+def turn_kernel(
+    own_ref, gate_ref, up_ref, down_ref, rows_ref, gate_t_ref, up_t_ref, far_ref, near_pre_ref, near_ref
+):
     core = this_core()
     first = core == 0
-    for j in range(CHIPS):
-        rows_ref[j, core] = own_ref[j]
-    for weight_ref, turned_ref in ((gate_ref, gate_t_ref), (up_ref, up_t_ref)):
-        for i in range(CHIPS // 2):
-            turned = weight_ref[0, :, pl.ds(i * 384, 384)].T
-            for half in range(2):
-                even = turned[192 * half : 192 * half + 96]
-                odd = turned[192 * half + 96 : 192 * half + 192]
-                turned_ref[0, 2 * i + half] = jnp.where(first, odd, even)
-                turned_ref[1, 2 * i + half] = jnp.where(first, even, odd)
+    for i in range(CHIPS):
+        rows_ref[chip_of(i, core), core] = own_ref[i // SIDE, i % SIDE]
+    for w, weight_ref in enumerate((gate_ref, up_ref, down_ref)):
+        for q in range(4):
+            wide = weight_ref[0, :, pl.ds(q * 768, 768)]
+            cut = [wide[:, 96 * p : 96 * p + 96] for p in range(8)]
+            even = jnp.concatenate(cut[0::2], axis=1)
+            odd = jnp.concatenate(cut[1::2], axis=1)
+            near = jnp.where(first, even, odd)
+            far = jnp.where(first, odd, even)
+            at = pl.ds(q * 384, 384)
+            near_ref[w, :, at] = near
+            far_ref[w, :, at] = far
+            if w < 2:
+                turned_ref = (gate_t_ref, up_t_ref)[w]
+                turned_ref[0, pl.ds(q * 4, 4)] = far.T.reshape(4, FEAT, HID)
+                turned_ref[1, pl.ds(q * 4, 4)] = near.T.reshape(4, FEAT, HID)
+    rows = rows_ref[:, core].reshape(D // 2, 640)
+    near_pre_ref[0] = dot(near_ref[0], rows[:, 0:384])
+    near_pre_ref[1] = dot(near_ref[1], rows[:, 0:384])
+    near_pre_ref[2] = dot(near_ref[2], rows[:, 256:640])
 
 
 def input_grads(turned, gate_t_ref, up_t_ref, grad_gate, grad_up, out_ref):
@@ -204,29 +227,18 @@
 
 
 def middle_kernel(
-    rows_in_ref,
-    other_ref,
-    gate_ref,
-    up_ref,
-    down_ref,
-    prob_ref,
-    gate_t_ref,
-    up_t_ref,
-    rows_ref,
-    send_ref,
-    score_ref,
-    hid_ref,
+    rows_in_ref, other_ref, far_ref, near_pre_ref, prob_ref, gate_t_ref, up_t_ref, rows_ref, send_ref, score_ref, hid_ref
 ):
     del rows_in_ref
     core = this_core()
-    for j in range(CHIPS):
-        rows_ref[j, 1 - core] = other_ref[j]
-    rows = rows_ref[...].reshape(D, 640)
+    for i in range(CHIPS):
+        rows_ref[chip_of(i, 1 - core), 1 - core] = other_ref[i // SIDE, i % SIDE]
+    rows = rows_ref[:, 1 - core].reshape(D // 2, 640)
     x_t = rows[:, 0:384]
     dy_t = rows[:, 256:640]
-    pre_gate = dot(gate_ref[0], x_t)
-    pre_up = dot(up_ref[0], x_t)
-    raw = dot(down_ref[0], dy_t)
+    pre_gate = near_pre_ref[0] + dot(far_ref[0], x_t)
+    pre_up = near_pre_ref[1] + dot(far_ref[1], x_t)
+    raw = near_pre_ref[2] + dot(far_ref[2], dy_t)
     back = jnp.concatenate([raw[:, 128:384], pltpu.roll(raw[:, 0:128], 64, 1)], axis=1)
     live = iota((1, WIDE), 1) < SLOTS
     back = jnp.where(live, back, 0.0)
@@ -308,6 +320,13 @@
 
 
 SAME_CORE = [[2 * j + core for j in range(CHIPS)] for core in range(2)]
+
+LINES = [
+    [[2 * (SIDE * y + x) for x in range(SIDE)] for y in range(SIDE)],
+    [[2 * (SIDE * y + x) + 1 for y in range(SIDE)] for x in range(SIDE)],
+    [[2 * (SIDE * y + x) for y in range(SIDE)] for x in range(SIDE)],
+    [[2 * (SIDE * y + x) + 1 for x in range(SIDE)] for y in range(SIDE)],
+]
 OTHER_CORE = [(i, i ^ 1) for i in range(2 * CHIPS)]
 
 
@@ -329,23 +348,33 @@
     got = lax.all_to_all(packed, "expert", 0, 0, tiled=True)
     copies, prob_rows = pl.pallas_call(
         spread_kernel,
-        out_shape=(struct(CHIPS, FEAT, 640, dtype=BF16), struct(8, WIDE, dtype=F32)),
+        out_shape=(struct(SIDE, FEAT, 640, dtype=BF16), struct(8, WIDE, dtype=F32)),
         compiler_params=params(16),
         name="spread",
     )(got)
-    own = lax.all_to_all(copies, "tensor", 0, 0, tiled=True, axis_index_groups=SAME_CORE)
+    line = lax.all_to_all(copies, "tensor", 0, 0, tiled=True, axis_index_groups=LINES[0] + LINES[1])
+    lines = pl.pallas_call(
+        relay_kernel,
+        out_shape=struct(SIDE, SIDE, FEAT, 640, dtype=BF16),
+        compiler_params=params(16),
+        name="relay",
+    )(line)
+    own = lax.all_to_all(lines, "tensor", 0, 0, tiled=True, axis_index_groups=LINES[2] + LINES[3])
     other = lax.ppermute(own, "tensor", OTHER_CORE)
-    rows, gate_t, up_t = pl.pallas_call(
+    rows, gate_t, up_t, far, near_pre = pl.pallas_call(
         turn_kernel,
         out_shape=(
             struct(CHIPS, 2, FEAT, 640, dtype=BF16),
             struct(2, CHIPS, FEAT, HID, dtype=BF16),
             struct(2, CHIPS, FEAT, HID, dtype=BF16),
+            struct(3, HID, D // 2, dtype=BF16),
+            struct(3, HID, WIDE, dtype=F32),
         ),
-        compiler_params=params(20),
+        scratch_shapes=[pltpu.VMEM((3, HID, D // 2), BF16)],
+        compiler_params=params(24),
         cost_estimate=cost(8e9),
         name="turn",
-    )(own, gate_weight, up_weight)
+    )(own, gate_weight, up_weight, down_weight)
     rows, send, score, hid = pl.pallas_call(
         middle_kernel,
         out_shape=(
@@ -358,7 +387,7 @@
         compiler_params=params(24),
         cost_estimate=cost(4e9),
         name="middle",
-    )(rows, other, gate_weight, up_weight, down_weight, prob_rows, gate_t, up_t)
+    )(rows, other, far, near_pre, prob_rows, gate_t, up_t)
     partner = lax.ppermute(send, "tensor", OTHER_CORE)
     keep, d_down = pl.pallas_call(
         rest_kernel,

time: 119 us -> 117 us (0.983)
  waiting for transfers between devices: 2.93 us -> 1.06 us
    all_to_all x1, blocking collectives: 20 us -> 17.6 us  [per_device(): back = lax.all_to_all(folded, 'expert', 0, 0, tiled=True)]
    ppermute x1, waiting for transfers between devices: 2.93 us -> 1.05 us  [per_device(): other = lax.ppermute(own, 'tensor', OTHER_CORE)]
    pallas_call x1, Pallas kernels: 0.98 us -> 2.85 us  [per_device(): pl.pallas_call(turn_kernel, out_shape=(struct(CHIPS, 2, FEAT, 640, dtype=...]
    all_to_all x1 -> x2, blocking collectives: 28.9 us -> 30.5 us  [the longest x1 18.5 us: per_device(): lax.all_to_all(lines, 'tensor', 0, 0, tiled=True, axis_index_groups=LINES...]
  transfers between devices with their start and end apart: 2 -> 2, of which waited for: 1 -> 1; matrix products, arithmetic and copies ran while one was open for 0% -> 0% of each run, Pallas kernels for 3% -> 5%
where the time goes in v2:
time: 117 us; the launch traced here: 116 us
  blocking collectives  98.2 us (84%)
  Pallas kernels  11.6 us (10%)
  starting transfers between devices  3.95 us (3%)
    all_to_all x1, blocking collectives, per_device(): got = lax.all_to_all(packed, 'expert', 0, 0, tiled=True)  29.7 us
    all_to_all x1, blocking collectives, per_device(): lax.all_to_all(joined, 'tensor', 0, 0, tiled=True, axis_index_groups=SAME...  20.4 us
    all_to_all x1, blocking collectives, per_device(): lax.all_to_all(lines, 'tensor', 0, 0, tiled=True, axis_index_groups=LINES...  18.5 us
    all_to_all x1, blocking collectives, per_device(): back = lax.all_to_all(folded, 'expert', 0, 0, tiled=True)  17.6 us
    all_to_all x1, blocking collectives, per_device(): lax.all_to_all(copies, 'tensor', 0, 0, tiled=True, axis_index_groups=LINE...  12 us
    pallas_call x1, Pallas kernels, per_device(): pl.pallas_call(turn_kernel, out_shape=(struct(CHIPS, 2, FEAT, 640, dtype=...  2.85 us
    pallas_call x1, Pallas kernels, per_device(): pl.pallas_call(rest_kernel, out_shape=(struct(CHIPS, 240, 128, dtype=F32)...  2.61 us
    pallas_call x1, Pallas kernels, per_device(): pl.pallas_call(middle_kernel, out_shape=(struct(CHIPS, 2, FEAT, 640, dtyp...  2.34 us
  transfers between devices with their start and end apart: 2, of which 1 were waited for; matrix products, arithmetic and copies ran while one was open for 0% of the time, Pallas kernels for 5%

profile of v2, /device:TPU:24, one launch (start us, length us, event | category | flops | bytes accessed | tf_op | source)
XLA Modules:
  0.0 115.5 jit_solution(4641191544711289194)
XLA Ops:
  0.6 1.6 %pack.1 = (bf16[16,32,128]{2,1,0:T(8,128)(2,1)S(1)}, s32[8,64]{1,0:T(8,128)S(1)}) custom-call(s32[4,64]{1,0:T(4,128)} %bitcast.3, bf16[4,64]{1,0:T(4,128)(2,1)} %bitcast.4, bf16[64,96]{1,0:T(8,128)(2,1)} %x_hbm.1, bf16[64,96]{1,0:T(8,128)(2,1)} %dy_hbm.1), custom_call_target="tpu_custom_call" | custom-call | tf_op jit(solution)/shard_map/pack/pallas_call | solution.py:334
  2.2 29.7 %all_to_all.25.got_ref = bf16[16,32,128]{2,1,0:T(8,128)(2,1)S(1)} all-to-all(bf16[16,32,128]{2,1,0:T(8,128)(2,1)S(1)} %get-tuple-element.20), channel_id=1, replica_groups=mesh['expert'=16,'tensor'=32] {'expert'}, dimensions={0} | all-to-all | bytes 262144 | tf_op jit(solution)/shard_map/all_to_all | solution.py:348
  31.9 0.6 spread.1
  32.5 12.0 %all_to_all.26.got_ref = bf16[4,96,640]{2,1,0:T(8,128)(2,1)S(1)} all-to-all(bf16[4,96,640]{2,1,0:T(8,128)(2,1)S(1)} %get-tuple-element.21), channel_id=1, replica_groups={{0,2,4,6},{8,10,12,14},{16,18,20,22},{24,26,28,30},{1,9,17,25},{3,11,19..., dimensions={0} | all-to-all | bytes 983040 | tf_op jit(solution)/shard_map/all_to_all | solution.py:355
  44.5 0.2 relay.1
  44.7 0.0 copy-start
  44.7 0.0 copy-start.1
  44.7 0.0 copy-start.2
  44.7 18.5 %all_to_all.27.own_ref = bf16[4,4,96,640]{3,2,1,0:T(8,128)(2,1)S(1)} all-to-all(bf16[4,4,96,640]{3,2,1,0:T(8,128)(2,1)S(1)} %relay.1), channel_id=1, replica_groups={{0,8,16,24},{2,10,18,26},{4,12,20,28},{6,14,22,30},{1,3,5,7},{9,11,13,1..., dimensions={0} | all-to-all | bytes 3932160 | tf_op jit(solution)/shard_map/all_to_all | solution.py:362
  63.2 1.9 %collective-permute-start = (bf16[4,4,96,640]{3,2,1,0:T(8,128)(2,1)S(1)}, bf16[4,4,96,640]{3,2,1,0:T(8,128)(2,1)S(1)}, u32[]{:S(2)}, u32[]{:S(2)}) collective-permute-start(bf16[4,4,96,640]{3,2,1,0:T(8,128)(2,1)S(1)} %all_to_all.27.own_ref), channel_id=1, source_target_pairs={{0,1},{1,0},{2,3},{3,2},{4,5},{5,4},{6,7},{7,6},{8,9},{9,8},{10,11... | collective-permute-start | bytes 5898248 | tf_op jit(solution)/shard_map/ppermute | solution.py:363
  65.1 0.0 copy-done
  65.1 0.0 copy-done.1
  65.1 0.0 copy-done.2
  65.1 2.9 %turn.1 = (bf16[16,2,96,640]{3,2,1,0:T(8,128)(2,1)S(1)}, bf16[2,16,96,168]{3,2,1,0:T(8,128)(2,1)S(1)}, bf16[2,16,96,168]{3,2,1,0:T(8,128)(2,1)S(1)}, bf16[3,168,1536]{2,1,0:T(8,128)(2,1)S(1)}, f32[3,168,384]{2,1,0:T(8,128)S(1)}) custom-call(bf16[4,4,96,640]{3,2,1,0:T(8,128)(2,1)S(1)} %all_to_all.27.own_ref, bf16[1,168,3072]{2,1,0:T(8,128)(2,1)S(1)} %copy-done, ...), custom_call_target="tpu_custom_call" | custom-call | flops 8000000000 | bytes 4194304 | tf_op jit(solution)/shard_map/turn/pallas_call | solution.py:364
  68.0 1.1 collective-permute-done.other_ref
  69.0 2.3 %middle.1 = (bf16[16,2,96,640]{3,2,1,0:T(8,128)(2,1)S(1)}, bf16[16,256,128]{2,1,0:T(8,128)(2,1)S(1)}, f32[16,128]{1,0:T(8,128)S(1)}, bf16[3,168,384]{2,1,0:T(8,128)(2,1)S(1)}) custom-call(bf16[16,2,96,640]{3,2,1,0:T(8,128)(2,1)S(1)} %get-tuple-element.22.rows_in_ref, ...), custom_call_target="tpu_custom_call", output_to_operand_aliasing={{0}: (0, {})} | custom-call | flops 4000000000 | bytes 4194304 | tf_op jit(solution)/shard_map/middle/pallas_call | solution.py:378
  71.4 2.0 %collective-permute-start.1 = (bf16[16,256,128]{2,1,0:T(8,128)(2,1)S(1)}, bf16[16,256,128]{2,1,0:T(8,128)(2,1)S(1)}, u32[]{:S(2)}, u32[]{:S(2)}) collective-permute-start(bf16[16,256,128]{2,1,0:T(8,128)(2,1)S(1)} %get-tuple-element.32), channel_id=1, source_target_pairs={{0,1},{1,0},{2,3},{3,2},{4,5},{5,4},{6,7},{7,6},{8,9},{9,8},{10,11... | collective-permute-start | bytes 3145736 | tf_op jit(solution)/shard_map/ppermute | solution.py:391
  73.4 2.6 %rest.1 = (f32[16,240,128]{2,1,0:T(8,128)S(1)}, bf16[1,168,3072]{2,1,0:T(8,128)(2,1)}) custom-call(bf16[16,2,96,640]{3,2,1,0:T(8,128)(2,1)S(1)} %get-tuple-element.28.rows_ref, bf16[3,168,384]{2,1,0:T(8,128)(2,1)S(1)} %get-tuple-element.29.hid_ref, bf16[2,16,96,168]{3,2,1,0:T(8,128)(2,1)S(1)} %get-tuple-element.26.gate_t_ref, ...), custom_call_target="tpu_custom_call" | custom-call | flops 4000000000 | bytes 4194304 | tf_op jit(solution)/shard_map/rest/pallas_call | solution.py:392
  76.0 0.0 collective-permute-done.1.got_ref
  76.0 0.2 join.1
  76.2 20.4 %all_to_all.28.got_ref = bf16[16,256,128]{2,1,0:T(8,128)(2,1)S(1)} all-to-all(bf16[16,256,128]{2,1,0:T(8,128)(2,1)S(1)} %join.1), channel_id=1, replica_groups={{0,2,4,6,8,10,12,14,16,18,20,22,24,26,28,30},{1,3,5,7,9,11,13,15,17,19,..., dimensions={0} | all-to-all | bytes 2097152 | tf_op jit(solution)/shard_map/all_to_all | solution.py:405
  96.6 0.4 fold.1
  97.0 17.6 %all_to_all.29.got_ref = bf16[16,32,128]{2,1,0:T(8,128)(2,1)S(1)} all-to-all(bf16[16,32,128]{2,1,0:T(8,128)(2,1)S(1)} %fold.1), channel_id=1, replica_groups=mesh['expert'=16,'tensor'=32] {'expert'}, dimensions={0} | all-to-all | bytes 262144 | tf_op jit(solution)/shard_map/all_to_all | solution.py:412
  114.6 0.9 combine.1
Async XLA Ops:
  44.7 20.4 %copy-start = (bf16[1,168,3072]{2,1,0:T(8,128)(2,1)S(1)}, bf16[1,168,3072]{2,1,0:T(8,128)(2,1)}, u32[]{:S(2)}) copy-start(bf16[1,168,3072]{2,1,0:T(8,128)(2,1)} %gate_ref.1) | copy-start | bytes 3096580
  44.7 20.4 %copy-start.1 = (bf16[1,168,3072]{2,1,0:T(8,128)(2,1)S(1)}, bf16[1,168,3072]{2,1,0:T(8,128)(2,1)}, u32[]{:S(2)}) copy-start(bf16[1,168,3072]{2,1,0:T(8,128)(2,1)} %up_ref.1) | copy-start | bytes 3096580
  44.7 20.4 %copy-start.2 = (bf16[1,168,3072]{2,1,0:T(8,128)(2,1)S(1)}, bf16[1,168,3072]{2,1,0:T(8,128)(2,1)}, u32[]{:S(2)}) copy-start(bf16[1,168,3072]{2,1,0:T(8,128)(2,1)} %down_ref.1) | copy-start | bytes 3096580
  63.2 5.9 %collective-permute-start = (bf16[4,4,96,640]{3,2,1,0:T(8,128)(2,1)S(1)}, bf16[4,4,96,640]{3,2,1,0:T(8,128)(2,1)S(1)}, u32[]{:S(2)}, u32[]{:S(2)}) collective-permute-start(bf16[4,4,96,640]{3,2,1,0:T(8,128)(2,1)S(1)} %all_to_all.27.own_ref), channel_id=1, source_target_pairs={{0,1},{1,0},{2,3},{3,2},{4,5},{5,4},{6,7},{7,6},{8,9},{9,8},{10,11... | collective-permute-start | bytes 5898248 | tf_op jit(solution)/shard_map/ppermute | solution.py:363
  71.4 4.7 %collective-permute-start.1 = (bf16[16,256,128]{2,1,0:T(8,128)(2,1)S(1)}, bf16[16,256,128]{2,1,0:T(8,128)(2,1)S(1)}, u32[]{:S(2)}, u32[]{:S(2)}) collective-permute-start(bf16[16,256,128]{2,1,0:T(8,128)(2,1)S(1)} %get-tuple-element.32), channel_id=1, source_target_pairs={{0,1},{1,0},{2,3},{3,2},{4,5},{5,4},{6,7},{7,6},{8,9},{9,8},{10,11... | collective-permute-start | bytes 3145736 | tf_op jit(solution)/shard_map/ppermute | solution.py:391

commit v3 on v2

--- a/solution.py
+++ b/solution.py
@@ -21,6 +21,7 @@
 HID = 168
 D = 3072
 BLOCK = 32
+BACK = 16
 
 
 def iota(shape, dim):
@@ -83,11 +84,10 @@
     rows = EXPERTS * BLOCK
     expand = hot(lax.shift_right_logical(iota((rows, EXPERTS), 0), 5) == iota((rows, EXPERTS), 1))
     place_rows = dot(expand, place.astype(BF16))
-    weight_rows = dot(expand, weight.astype(BF16))
     s_int = iota((rows, TOK), 0) & (BLOCK - 1)
     s = s_int.astype(F32)
     tail = (s_int >= CAP) & (s_int < 30)
-    main = flag((place_rows == s) & (s_int < CAP))
+    main = hot((place_rows == s) & (s_int < CAP))
     left = hot((place_rows == s - 20.0) & tail)
     right = hot((place_rows == s - 10.0) & tail)
 
@@ -99,15 +99,16 @@
     b_left = dot(dy, hot((lane == f - 32) & (f >= 32)))
     b_right = dot(dy, hot((lane == f + 32) & (f >= 32)))
 
-    prob_col = jnp.sum(main * weight_rows, axis=1, keepdims=True)
-    s_lane = iota((rows, 128), 0) & (BLOCK - 1)
-    prob_wide = jnp.where(s_lane == iota((rows, 128), 1), prob_col, 0.0).astype(BF16)
-    gather = hot(lax.shift_right_logical(iota((EXPERTS, rows), 1), 5) == iota((EXPERTS, rows), 0))
-    prob_block = dot(gather, prob_wide).astype(BF16)
+    lane_e = iota((EXPERTS, 128), 1)
+    prob_block = jnp.zeros((EXPERTS, 128), F32)
+    for j in range(CAP):
+        column = jnp.sum(jnp.where(place == float(j), weight, 0.0), axis=1, keepdims=True)
+        prob_block = jnp.where(lane_e == j, column, prob_block)
+    prob_block = prob_block.astype(BF16)
     at_30 = hot(iota((rows, EXPERTS), 0) == iota((rows, EXPERTS), 1) * BLOCK + 30)
 
     out = (
-        dot(main.astype(BF16), b_main.astype(BF16))
+        dot(main, b_main.astype(BF16))
         + dot(left, b_left.astype(BF16))
         + dot(right, b_right.astype(BF16))
         + dot(at_30, prob_block)
@@ -292,27 +293,48 @@
     wide = jnp.concatenate([score[0:1], score[1:2], score[2:3]], axis=1)
     high = wide.astype(BF16).astype(F32)
     low = wide - high
-    row = iota((32, WIDE), 0)
-    extra = jnp.where(row == 0, high, 0.0) + jnp.where(row == 1, low, 0.0)
-    table = jnp.concatenate([grads, extra], axis=0).astype(BF16)
     n = iota((1, WIDE), 1)
     e = expert_of(n)
-    to = jnp.where(n < SLOTS, e * BLOCK + (n - e * CAP), -1)
-    pick = hot(iota((EXPERTS * BLOCK, WIDE), 0) == to)
-    out_ref[...] = dot_last(pick, table).astype(BF16).reshape(EXPERTS, BLOCK, 128)
+    slot = n - e * CAP
+    base = jnp.where(n < SLOTS, e * BACK, -2 * BACK)
+    r = iota((EXPERTS * BACK, WIDE), 0)
+    upper = jnp.concatenate([grads, jnp.zeros((32, WIDE), F32)], axis=0).astype(BF16)
+    out = dot_last(hot((r == base + slot) & (slot < BACK)), upper)
+    for q in range(3):
+        part = jnp.concatenate([jnp.zeros((FEAT, WIDE), F32), grads[32 * q : 32 * q + 32]], axis=0).astype(BF16)
+        out = out + dot_last(hot((r == base + 3 * (slot - BACK) + q) & (slot >= BACK)), part)
+    values = jnp.where(r == base + 12, high, 0.0) + jnp.where(r == base + 13, low, 0.0)
+    out = out + dot_last(values.astype(BF16), hot(iota((128, WIDE), 0) == slot + FEAT))
+    out_ref[...] = out.astype(BF16).reshape(EXPERTS, BACK, 128)
 
 
 def combine_kernel(got_ref, row_ref, d_tokens_ref, d_probs_ref):
-    rows = EXPERTS * BLOCK
+    rows = EXPERTS * BACK
     got = got_ref[...].reshape(rows, 128)
     r = iota((rows, TOK), 0)
-    picks = [flag(r == row_ref[k : k + 1, :]) for k in range(TOP)]
-    d_tokens_ref[...] = dot_first(sum(picks).astype(BF16), got)[:, 0:FEAT].astype(BF16)
-    lane = iota((rows, 128), 1)
-    score = jnp.where((lane == 96) | (lane == 97), got.astype(F32), 0.0)
-    score = jnp.sum(score, axis=1, keepdims=True)
+    lane = iota((128, TOK), 0)
+    pick = jnp.zeros((rows, TOK), F32)
+    rest = [jnp.zeros((rows, TOK), F32) for _ in range(3)]
+    own = iota((EXPERTS, rows), 1) - iota((EXPERTS, rows), 0) * BACK
+    high = dot(hot(own == 12), got).astype(BF16)
+    low = dot(hot(own == 13), got).astype(BF16)
     for k in range(TOP):
-        d_probs_ref[k : k + 1, :] = jnp.sum(picks[k] * score, axis=0, keepdims=True)
+        at = row_ref[k : k + 1, :]
+        e = lax.shift_right_logical(at, 5)
+        slot = at & (BLOCK - 1)
+        base = e * BACK
+        pick = pick + flag((r == base + slot) & (slot < BACK))
+        for q in range(3):
+            rest[q] = rest[q] + flag((r == base + 3 * (slot - BACK) + q) & (slot >= BACK))
+        mine = hot(iota((EXPERTS, TOK), 0) == e)
+        score = dot_first(high, mine) + dot_first(low, mine)
+        d_probs_ref[k : k + 1, :] = jnp.sum(jnp.where(lane == slot + FEAT, score, 0.0), axis=0, keepdims=True)
+    total = dot_first(pick.astype(BF16), got)
+    feature = iota((TOK, 128), 1)
+    for q in range(3):
+        part = pltpu.roll(dot_first(rest[q].astype(BF16), got), 32 + 32 * q, 1)
+        total = total + jnp.where(lax.shift_right_logical(feature, 5) == q, part, 0.0)
+    d_tokens_ref[...] = total[:, 0:FEAT].astype(BF16)
 
 
 def struct(*shape, dtype):
@@ -405,7 +427,7 @@
     shares = lax.all_to_all(joined, "tensor", 0, 0, tiled=True, axis_index_groups=SAME_CORE)
     folded = pl.pallas_call(
         fold_kernel,
-        out_shape=struct(EXPERTS, BLOCK, 128, dtype=BF16),
+        out_shape=struct(EXPERTS, BACK, 128, dtype=BF16),
         compiler_params=params(16),
         name="fold",
     )(shares)

time: 117 us -> 116 us (level)
  blocking collectives: 98.2 us -> 96.7 us
    all_to_all x1, blocking collectives: 17.6 us -> 16.2 us  [per_device(): back = lax.all_to_all(folded, 'expert', 0, 0, tiled=True)]
where the time goes in v3:
time: 116 us; the launch traced here: 114 us
  blocking collectives  96.7 us (83%)
  Pallas kernels  11.9 us (10%)
  starting transfers between devices  3.95 us (3%)
    all_to_all x1, blocking collectives, per_device(): got = lax.all_to_all(packed, 'expert', 0, 0, tiled=True)  29.7 us
    all_to_all x1, blocking collectives, per_device(): lax.all_to_all(joined, 'tensor', 0, 0, tiled=True, axis_index_groups=SAME...  20.4 us
    all_to_all x1, blocking collectives, per_device(): lax.all_to_all(lines, 'tensor', 0, 0, tiled=True, axis_index_groups=LINES...  18.5 us
    all_to_all x1, blocking collectives, per_device(): back = lax.all_to_all(folded, 'expert', 0, 0, tiled=True)  16.2 us
    all_to_all x1, blocking collectives, per_device(): lax.all_to_all(copies, 'tensor', 0, 0, tiled=True, axis_index_groups=LINE...  12 us
    pallas_call x1, Pallas kernels, per_device(): pl.pallas_call(turn_kernel, out_shape=(struct(CHIPS, 2, FEAT, 640, dtype=...  2.84 us
    pallas_call x1, Pallas kernels, per_device(): pl.pallas_call(rest_kernel, out_shape=(struct(CHIPS, 240, 128, dtype=F32)...  2.61 us
    pallas_call x1, Pallas kernels, per_device(): pl.pallas_call(middle_kernel, out_shape=(struct(CHIPS, 2, FEAT, 640, dtyp...  2.34 us
  transfers between devices with their start and end apart: 2, of which 1 were waited for; matrix products, arithmetic and copies ran while one was open for 0% of the time, Pallas kernels for 5%

profile of v3, /device:TPU:24, one launch (start us, length us, event | category | flops | bytes accessed | tf_op | source)
XLA Modules:
  0.0 114.4 jit_solution(7473967803338329098)
XLA Ops:
  0.6 1.3 %pack.1 = (bf16[16,32,128]{2,1,0:T(8,128)(2,1)S(1)}, s32[8,64]{1,0:T(8,128)S(1)}) custom-call(s32[4,64]{1,0:T(4,128)} %bitcast.3, bf16[4,64]{1,0:T(4,128)(2,1)} %bitcast.4, bf16[64,96]{1,0:T(8,128)(2,1)} %x_hbm.1, bf16[64,96]{1,0:T(8,128)(2,1)} %dy_hbm.1), custom_call_target="tpu_custom_call" | custom-call | tf_op jit(solution)/shard_map/pack/pallas_call | solution.py:356
  2.0 29.7 %all_to_all.25.got_ref = bf16[16,32,128]{2,1,0:T(8,128)(2,1)S(1)} all-to-all(bf16[16,32,128]{2,1,0:T(8,128)(2,1)S(1)} %get-tuple-element.20), channel_id=1, replica_groups=mesh['expert'=16,'tensor'=32] {'expert'}, dimensions={0} | all-to-all | bytes 262144 | tf_op jit(solution)/shard_map/all_to_all | solution.py:370
  31.7 0.6 spread.1
  32.3 12.0 %all_to_all.26.got_ref = bf16[4,96,640]{2,1,0:T(8,128)(2,1)S(1)} all-to-all(bf16[4,96,640]{2,1,0:T(8,128)(2,1)S(1)} %get-tuple-element.21), channel_id=1, replica_groups={{0,2,4,6},{8,10,12,14},{16,18,20,22},{24,26,28,30},{1,9,17,25},{3,11,19..., dimensions={0} | all-to-all | bytes 983040 | tf_op jit(solution)/shard_map/all_to_all | solution.py:377
  44.3 0.2 relay.1
  44.4 0.0 copy-start
  44.5 0.0 copy-start.1
  44.5 0.0 copy-start.2
  44.5 18.5 %all_to_all.27.own_ref = bf16[4,4,96,640]{3,2,1,0:T(8,128)(2,1)S(1)} all-to-all(bf16[4,4,96,640]{3,2,1,0:T(8,128)(2,1)S(1)} %relay.1), channel_id=1, replica_groups={{0,8,16,24},{2,10,18,26},{4,12,20,28},{6,14,22,30},{1,3,5,7},{9,11,13,1..., dimensions={0} | all-to-all | bytes 3932160 | tf_op jit(solution)/shard_map/all_to_all | solution.py:384
  63.0 1.9 %collective-permute-start = (bf16[4,4,96,640]{3,2,1,0:T(8,128)(2,1)S(1)}, bf16[4,4,96,640]{3,2,1,0:T(8,128)(2,1)S(1)}, u32[]{:S(2)}, u32[]{:S(2)}) collective-permute-start(bf16[4,4,96,640]{3,2,1,0:T(8,128)(2,1)S(1)} %all_to_all.27.own_ref), channel_id=1, source_target_pairs={{0,1},{1,0},{2,3},{3,2},{4,5},{5,4},{6,7},{7,6},{8,9},{9,8},{10,11... | collective-permute-start | bytes 5898248 | tf_op jit(solution)/shard_map/ppermute | solution.py:385
  64.9 0.0 copy-done
  64.9 0.0 copy-done.1
  64.9 0.0 copy-done.2
  64.9 2.8 %turn.1 = (bf16[16,2,96,640]{3,2,1,0:T(8,128)(2,1)S(1)}, bf16[2,16,96,168]{3,2,1,0:T(8,128)(2,1)S(1)}, bf16[2,16,96,168]{3,2,1,0:T(8,128)(2,1)S(1)}, bf16[3,168,1536]{2,1,0:T(8,128)(2,1)S(1)}, f32[3,168,384]{2,1,0:T(8,128)S(1)}) custom-call(bf16[4,4,96,640]{3,2,1,0:T(8,128)(2,1)S(1)} %all_to_all.27.own_ref, bf16[1,168,3072]{2,1,0:T(8,128)(2,1)S(1)} %copy-done, ...), custom_call_target="tpu_custom_call" | custom-call | flops 8000000000 | bytes 4194304 | tf_op jit(solution)/shard_map/turn/pallas_call | solution.py:386
  67.8 1.1 collective-permute-done.other_ref
  68.8 2.3 %middle.1 = (bf16[16,2,96,640]{3,2,1,0:T(8,128)(2,1)S(1)}, bf16[16,256,128]{2,1,0:T(8,128)(2,1)S(1)}, f32[16,128]{1,0:T(8,128)S(1)}, bf16[3,168,384]{2,1,0:T(8,128)(2,1)S(1)}) custom-call(bf16[16,2,96,640]{3,2,1,0:T(8,128)(2,1)S(1)} %get-tuple-element.22.rows_in_ref, ...), custom_call_target="tpu_custom_call", output_to_operand_aliasing={{0}: (0, {})} | custom-call | flops 4000000000 | bytes 4194304 | tf_op jit(solution)/shard_map/middle/pallas_call | solution.py:400
  71.2 2.0 %collective-permute-start.1 = (bf16[16,256,128]{2,1,0:T(8,128)(2,1)S(1)}, bf16[16,256,128]{2,1,0:T(8,128)(2,1)S(1)}, u32[]{:S(2)}, u32[]{:S(2)}) collective-permute-start(bf16[16,256,128]{2,1,0:T(8,128)(2,1)S(1)} %get-tuple-element.32), channel_id=1, source_target_pairs={{0,1},{1,0},{2,3},{3,2},{4,5},{5,4},{6,7},{7,6},{8,9},{9,8},{10,11... | collective-permute-start | bytes 3145736 | tf_op jit(solution)/shard_map/ppermute | solution.py:413
  73.2 2.6 %rest.1 = (f32[16,240,128]{2,1,0:T(8,128)S(1)}, bf16[1,168,3072]{2,1,0:T(8,128)(2,1)}) custom-call(bf16[16,2,96,640]{3,2,1,0:T(8,128)(2,1)S(1)} %get-tuple-element.28.rows_ref, bf16[3,168,384]{2,1,0:T(8,128)(2,1)S(1)} %get-tuple-element.29.hid_ref, bf16[2,16,96,168]{3,2,1,0:T(8,128)(2,1)S(1)} %get-tuple-element.26.gate_t_ref, ...), custom_call_target="tpu_custom_call" | custom-call | flops 4000000000 | bytes 4194304 | tf_op jit(solution)/shard_map/rest/pallas_call | solution.py:414
  75.8 0.0 collective-permute-done.1.got_ref
  75.8 0.2 join.1
  76.0 20.4 %all_to_all.28.got_ref = bf16[16,256,128]{2,1,0:T(8,128)(2,1)S(1)} all-to-all(bf16[16,256,128]{2,1,0:T(8,128)(2,1)S(1)} %join.1), channel_id=1, replica_groups={{0,2,4,6,8,10,12,14,16,18,20,22,24,26,28,30},{1,3,5,7,9,11,13,15,17,19,..., dimensions={0} | all-to-all | bytes 2097152 | tf_op jit(solution)/shard_map/all_to_all | solution.py:427
  96.4 0.6 fold.1
  97.0 16.2 %all_to_all.29.got_ref = bf16[16,16,128]{2,1,0:T(8,128)(2,1)S(1)} all-to-all(bf16[16,16,128]{2,1,0:T(8,128)(2,1)S(1)} %fold.1), channel_id=1, replica_groups=mesh['expert'=16,'tensor'=32] {'expert'}, dimensions={0} | all-to-all | bytes 131072 | tf_op jit(solution)/shard_map/all_to_all | solution.py:434
  113.2 1.2 %combine.1 = (bf16[64,96]{1,0:T(8,128)(2,1)}, f32[4,64]{1,0:T(4,128)}) custom-call(bf16[16,16,128]{2,1,0:T(8,128)(2,1)S(1)} %all_to_all.29.got_ref, s32[8,64]{1,0:T(8,128)S(1)} %get-tuple-element.33.row_ref), custom_call_target="tpu_custom_call" | custom-call | tf_op jit(solution)/shard_map/combine/pallas_call | solution.py:435
Async XLA Ops:
  44.4 20.4 %copy-start = (bf16[1,168,3072]{2,1,0:T(8,128)(2,1)S(1)}, bf16[1,168,3072]{2,1,0:T(8,128)(2,1)}, u32[]{:S(2)}) copy-start(bf16[1,168,3072]{2,1,0:T(8,128)(2,1)} %gate_ref.1) | copy-start | bytes 3096580
  44.5 20.4 %copy-start.1 = (bf16[1,168,3072]{2,1,0:T(8,128)(2,1)S(1)}, bf16[1,168,3072]{2,1,0:T(8,128)(2,1)}, u32[]{:S(2)}) copy-start(bf16[1,168,3072]{2,1,0:T(8,128)(2,1)} %up_ref.1) | copy-start | bytes 3096580
  44.5 20.4 %copy-start.2 = (bf16[1,168,3072]{2,1,0:T(8,128)(2,1)S(1)}, bf16[1,168,3072]{2,1,0:T(8,128)(2,1)}, u32[]{:S(2)}) copy-start(bf16[1,168,3072]{2,1,0:T(8,128)(2,1)} %down_ref.1) | copy-start | bytes 3096580
  63.0 5.9 %collective-permute-start = (bf16[4,4,96,640]{3,2,1,0:T(8,128)(2,1)S(1)}, bf16[4,4,96,640]{3,2,1,0:T(8,128)(2,1)S(1)}, u32[]{:S(2)}, u32[]{:S(2)}) collective-permute-start(bf16[4,4,96,640]{3,2,1,0:T(8,128)(2,1)S(1)} %all_to_all.27.own_ref), channel_id=1, source_target_pairs={{0,1},{1,0},{2,3},{3,2},{4,5},{5,4},{6,7},{7,6},{8,9},{9,8},{10,11... | collective-permute-start | bytes 5898248 | tf_op jit(solution)/shard_map/ppermute | solution.py:385
  71.2 4.7 %collective-permute-start.1 = (bf16[16,256,128]{2,1,0:T(8,128)(2,1)S(1)}, bf16[16,256,128]{2,1,0:T(8,128)(2,1)S(1)}, u32[]{:S(2)}, u32[]{:S(2)}) collective-permute-start(bf16[16,256,128]{2,1,0:T(8,128)(2,1)S(1)} %get-tuple-element.32), channel_id=1, source_target_pairs={{0,1},{1,0},{2,3},{3,2},{4,5},{5,4},{6,7},{7,6},{8,9},{9,8},{10,11... | collective-permute-start | bytes 3145736 | tf_op jit(solution)/shard_map/ppermute | solution.py:413

commit v4 on v3

--- a/solution.py
+++ b/solution.py
@@ -1,5 +1,7 @@
 import jax
 import jax.numpy as jnp
+import ml_dtypes
+import numpy as np
 from jax import lax
 from jax.experimental import pallas as pl
 from jax.experimental.pallas import tpu as pltpu
@@ -116,6 +118,16 @@
     out_ref[...] = out.astype(BF16).reshape(EXPERTS, BLOCK, 128)
 
 
+def fold_table():
+    n = np.arange(WIDE)
+    r = np.arange(EXPERTS * BACK)[:, None]
+    e, s = n // CAP, n % CAP
+    masks = [(r == e * BACK + s) & (s < BACK)]
+    masks += [(r == e * BACK + 3 * (s - BACK) + q) & (s >= BACK) for q in range(3)]
+    masks += [r == e * BACK + 12, r == e * BACK + 13]
+    return (np.stack(masks) & (n < SLOTS)).astype(ml_dtypes.bfloat16)
+
+
 def spread_kernel(got_ref, out_ref, prob_ref):
     rows = EXPERTS * BLOCK
     got = got_ref[...].reshape(rows, 128)
@@ -131,10 +143,13 @@
     to_left = jnp.where(live & (s_d < 10), e_d * BLOCK + 20 + s_d, -1)
     to_right = jnp.where(live & (s_d >= 10), e_d * BLOCK + 10 + s_d, -1)
     r = iota((rows, WIDE), 0)
-    part_x = dot_first(got, hot(r == to_x))
-    part_d = dot_first(got, hot(r == to_d))
-    part_l = dot_first(got, hot(r == to_left))
-    part_r = dot_first(got, hot(r == to_right))
+    got_t = got.T
+    part_x = dot(got_t, hot(r == to_x))
+    part_d = dot(got_t, hot(r == to_d))
+    both = hot(r == to_left + to_right + 1)
+    mixed = dot(got_t, both)
+    part_l = jnp.where(s_d < 10, mixed, 0.0)
+    part_r = jnp.where(s_d < 10, 0.0, mixed)
     x_t = part_x[0:FEAT]
     d_t = jnp.concatenate([part_d[96:128], part_l[0:64] + part_r[64:128]], axis=0)
     first = x_t[:, 0:256].astype(BF16)
@@ -187,8 +202,36 @@
     return jnp.where(core == 0, i, (i % SIDE) * SIDE + i // SIDE)
 
 
+def pick_routes(row_ref, pick_ref):
+    places = row_ref[...].astype(F32).T.astype(I32)
+    r = iota((TOK, EXPERTS * BACK), 1)
+    picks = [jnp.zeros(r.shape, F32)] * 4
+    for k in range(TOP):
+        at = places[:, k : k + 1]
+        slot = at & (BLOCK - 1)
+        base = lax.shift_right_logical(at, 5) * BACK
+        first = jnp.where(slot < BACK, base + slot, -1)
+        later = jnp.where(slot < BACK, -3, base + 3 * (slot - BACK))
+        picks[0] = picks[0] + flag(r == first)
+        for q in range(3):
+            picks[1 + q] = picks[1 + q] + flag(r == later + q)
+    for q in range(4):
+        pick_ref[q] = picks[q].astype(BF16)
+
+
 def turn_kernel(
-    own_ref, gate_ref, up_ref, down_ref, rows_ref, gate_t_ref, up_t_ref, far_ref, near_pre_ref, near_ref
+    own_ref,
+    gate_ref,
+    up_ref,
+    down_ref,
+    row_ref,
+    rows_ref,
+    gate_t_ref,
+    up_t_ref,
+    far_ref,
+    near_pre_ref,
+    pick_ref,
+    near_ref,
 ):
     core = this_core()
     first = core == 0
@@ -213,6 +256,7 @@
     near_pre_ref[0] = dot(near_ref[0], rows[:, 0:384])
     near_pre_ref[1] = dot(near_ref[1], rows[:, 0:384])
     near_pre_ref[2] = dot(near_ref[2], rows[:, 256:640])
+    pick_routes(row_ref, pick_ref)
 
 
 def input_grads(turned, gate_t_ref, up_t_ref, grad_gate, grad_up, out_ref):
@@ -278,7 +322,7 @@
         out_ref[j, 240:256] = parts
 
 
-def fold_kernel(got_ref, out_ref):
+def fold_kernel(got_ref, table_ref, out_ref):
     total = got_ref[0].astype(F32)
     for j in range(1, CHIPS):
         total = total + got_ref[j].astype(F32)
@@ -296,45 +340,35 @@
     n = iota((1, WIDE), 1)
     e = expert_of(n)
     slot = n - e * CAP
-    base = jnp.where(n < SLOTS, e * BACK, -2 * BACK)
-    r = iota((EXPERTS * BACK, WIDE), 0)
     upper = jnp.concatenate([grads, jnp.zeros((32, WIDE), F32)], axis=0).astype(BF16)
-    out = dot_last(hot((r == base + slot) & (slot < BACK)), upper)
+    out = dot_last(table_ref[0], upper)
     for q in range(3):
         part = jnp.concatenate([jnp.zeros((FEAT, WIDE), F32), grads[32 * q : 32 * q + 32]], axis=0).astype(BF16)
-        out = out + dot_last(hot((r == base + 3 * (slot - BACK) + q) & (slot >= BACK)), part)
-    values = jnp.where(r == base + 12, high, 0.0) + jnp.where(r == base + 13, low, 0.0)
+        out = out + dot_last(table_ref[1 + q], part)
+    values = table_ref[4].astype(F32) * high + table_ref[5].astype(F32) * low
     out = out + dot_last(values.astype(BF16), hot(iota((128, WIDE), 0) == slot + FEAT))
     out_ref[...] = out.astype(BF16).reshape(EXPERTS, BACK, 128)
 
 
-def combine_kernel(got_ref, row_ref, d_tokens_ref, d_probs_ref):
+def combine_kernel(got_ref, row_ref, pick_ref, d_tokens_ref, d_probs_ref):
     rows = EXPERTS * BACK
     got = got_ref[...].reshape(rows, 128)
-    r = iota((rows, TOK), 0)
+    total = dot(pick_ref[0], got)
+    feature = iota((TOK, 128), 1)
+    for q in range(3):
+        part = pltpu.roll(dot(pick_ref[1 + q], got), 32 + 32 * q, 1)
+        total = total + jnp.where(lax.shift_right_logical(feature, 5) == q, part, 0.0)
+    d_tokens_ref[...] = total[:, 0:FEAT].astype(BF16)
     lane = iota((128, TOK), 0)
-    pick = jnp.zeros((rows, TOK), F32)
-    rest = [jnp.zeros((rows, TOK), F32) for _ in range(3)]
     own = iota((EXPERTS, rows), 1) - iota((EXPERTS, rows), 0) * BACK
     high = dot(hot(own == 12), got).astype(BF16)
     low = dot(hot(own == 13), got).astype(BF16)
     for k in range(TOP):
         at = row_ref[k : k + 1, :]
-        e = lax.shift_right_logical(at, 5)
-        slot = at & (BLOCK - 1)
-        base = e * BACK
-        pick = pick + flag((r == base + slot) & (slot < BACK))
-        for q in range(3):
-            rest[q] = rest[q] + flag((r == base + 3 * (slot - BACK) + q) & (slot >= BACK))
-        mine = hot(iota((EXPERTS, TOK), 0) == e)
+        mine = hot(iota((EXPERTS, TOK), 0) == lax.shift_right_logical(at, 5))
         score = dot_first(high, mine) + dot_first(low, mine)
-        d_probs_ref[k : k + 1, :] = jnp.sum(jnp.where(lane == slot + FEAT, score, 0.0), axis=0, keepdims=True)
-    total = dot_first(pick.astype(BF16), got)
-    feature = iota((TOK, 128), 1)
-    for q in range(3):
-        part = pltpu.roll(dot_first(rest[q].astype(BF16), got), 32 + 32 * q, 1)
-        total = total + jnp.where(lax.shift_right_logical(feature, 5) == q, part, 0.0)
-    d_tokens_ref[...] = total[:, 0:FEAT].astype(BF16)
+        column = (at & (BLOCK - 1)) + FEAT
+        d_probs_ref[k : k + 1, :] = jnp.sum(jnp.where(lane == column, score, 0.0), axis=0, keepdims=True)
 
 
 def struct(*shape, dtype):
@@ -383,7 +417,7 @@
     )(line)
     own = lax.all_to_all(lines, "tensor", 0, 0, tiled=True, axis_index_groups=LINES[2] + LINES[3])
     other = lax.ppermute(own, "tensor", OTHER_CORE)
-    rows, gate_t, up_t, far, near_pre = pl.pallas_call(
+    rows, gate_t, up_t, far, near_pre, picks = pl.pallas_call(
         turn_kernel,
         out_shape=(
             struct(CHIPS, 2, FEAT, 640, dtype=BF16),
@@ -391,12 +425,13 @@
             struct(2, CHIPS, FEAT, HID, dtype=BF16),
             struct(3, HID, D // 2, dtype=BF16),
             struct(3, HID, WIDE, dtype=F32),
+            struct(4, TOK, EXPERTS * BACK, dtype=BF16),
         ),
         scratch_shapes=[pltpu.VMEM((3, HID, D // 2), BF16)],
         compiler_params=params(24),
         cost_estimate=cost(8e9),
         name="turn",
-    )(own, gate_weight, up_weight, down_weight)
+    )(own, gate_weight, up_weight, down_weight, row_of)
     rows, send, score, hid = pl.pallas_call(
         middle_kernel,
         out_shape=(
@@ -430,14 +465,14 @@
         out_shape=struct(EXPERTS, BACK, 128, dtype=BF16),
         compiler_params=params(16),
         name="fold",
-    )(shares)
+    )(shares, jnp.asarray(fold_table()))
     back = lax.all_to_all(folded, "expert", 0, 0, tiled=True)
     d_tokens, d_probs = pl.pallas_call(
         combine_kernel,
         out_shape=(struct(TOK, FEAT, dtype=BF16), struct(TOP, TOK, dtype=F32)),
         compiler_params=params(16),
         name="combine",
-    )(back, row_of)
+    )(back, row_of, picks)
     return d_tokens, d_probs.T, d_down
 
 

time: 116 us -> 116 us (level)
  no operation moved by 1% of the time
where the time goes in v4:
time: 116 us; the launch traced here: 114 us
  blocking collectives  96.9 us (84%)
  Pallas kernels  11.7 us (10%)
  starting transfers between devices  3.94 us (3%)
    all_to_all x1, blocking collectives, per_device(): got = lax.all_to_all(packed, 'expert', 0, 0, tiled=True)  29.7 us
    all_to_all x1, blocking collectives, per_device(): lax.all_to_all(joined, 'tensor', 0, 0, tiled=True, axis_index_groups=SAME...  20.5 us
    all_to_all x1, blocking collectives, per_device(): lax.all_to_all(lines, 'tensor', 0, 0, tiled=True, axis_index_groups=LINES...  18.5 us
    all_to_all x1, blocking collectives, per_device(): back = lax.all_to_all(folded, 'expert', 0, 0, tiled=True)  16.2 us
    all_to_all x1, blocking collectives, per_device(): lax.all_to_all(copies, 'tensor', 0, 0, tiled=True, axis_index_groups=LINE...  12 us
    pallas_call x1, Pallas kernels, per_device(): pl.pallas_call(turn_kernel, out_shape=(struct(CHIPS, 2, FEAT, 640, dtype=...  3.08 us
    pallas_call x1, Pallas kernels, per_device(): pl.pallas_call(rest_kernel, out_shape=(struct(CHIPS, 240, 128, dtype=F32)...  2.6 us
    pallas_call x1, Pallas kernels, per_device(): pl.pallas_call(middle_kernel, out_shape=(struct(CHIPS, 2, FEAT, 640, dtyp...  2.35 us
  transfers between devices with their start and end apart: 2, of which 1 were waited for; matrix products, arithmetic and copies ran while one was open for 0% of the time, Pallas kernels for 5%

profile of v4, /device:TPU:24, one launch (start us, length us, event | category | flops | bytes accessed | tf_op | source)
XLA Modules:
  0.0 114.1 jit_solution(13878780126856137964)
XLA Ops:
  0.6 1.3 %pack.1 = (bf16[16,32,128]{2,1,0:T(8,128)(2,1)S(1)}, s32[8,64]{1,0:T(8,128)S(1)}) custom-call(s32[4,64]{1,0:T(4,128)} %bitcast.3, bf16[4,64]{1,0:T(4,128)(2,1)} %bitcast.4, bf16[64,96]{1,0:T(8,128)(2,1)} %x_hbm.1, bf16[64,96]{1,0:T(8,128)(2,1)} %dy_hbm.1), custom_call_target="tpu_custom_call" | custom-call | tf_op jit(solution)/shard_map/pack/pallas_call | solution.py:390
  2.0 29.7 %all_to_all.25.got_ref = bf16[16,32,128]{2,1,0:T(8,128)(2,1)S(1)} all-to-all(bf16[16,32,128]{2,1,0:T(8,128)(2,1)S(1)} %get-tuple-element.21), channel_id=1, replica_groups=mesh['expert'=16,'tensor'=32] {'expert'}, dimensions={0} | all-to-all | bytes 262144 | tf_op jit(solution)/shard_map/all_to_all | solution.py:404
  31.7 0.5 spread.1
  32.2 12.0 %all_to_all.26.got_ref = bf16[4,96,640]{2,1,0:T(8,128)(2,1)S(1)} all-to-all(bf16[4,96,640]{2,1,0:T(8,128)(2,1)S(1)} %get-tuple-element.22), channel_id=1, replica_groups={{0,2,4,6},{8,10,12,14},{16,18,20,22},{24,26,28,30},{1,9,17,25},{3,11,19..., dimensions={0} | all-to-all | bytes 983040 | tf_op jit(solution)/shard_map/all_to_all | solution.py:411
  44.2 0.2 relay.1
  44.4 0.0 copy-start.1
  44.4 0.0 copy-start.2
  44.4 0.0 copy-start.3
  44.4 18.5 %all_to_all.27.own_ref = bf16[4,4,96,640]{3,2,1,0:T(8,128)(2,1)S(1)} all-to-all(bf16[4,4,96,640]{3,2,1,0:T(8,128)(2,1)S(1)} %relay.1), channel_id=1, replica_groups={{0,8,16,24},{2,10,18,26},{4,12,20,28},{6,14,22,30},{1,3,5,7},{9,11,13,1..., dimensions={0} | all-to-all | bytes 3932160 | tf_op jit(solution)/shard_map/all_to_all | solution.py:418
  62.9 1.9 %collective-permute-start = (bf16[4,4,96,640]{3,2,1,0:T(8,128)(2,1)S(1)}, bf16[4,4,96,640]{3,2,1,0:T(8,128)(2,1)S(1)}, u32[]{:S(2)}, u32[]{:S(2)}) collective-permute-start(bf16[4,4,96,640]{3,2,1,0:T(8,128)(2,1)S(1)} %all_to_all.27.own_ref), channel_id=1, source_target_pairs={{0,1},{1,0},{2,3},{3,2},{4,5},{5,4},{6,7},{7,6},{8,9},{9,8},{10,11... | collective-permute-start | bytes 5898248 | tf_op jit(solution)/shard_map/ppermute | solution.py:419
  64.8 0.0 copy-done.1
  64.8 0.0 copy-done.2
  64.8 0.0 copy-done.3
  64.8 3.1 %turn.1 = (bf16[16,2,96,640]{3,2,1,0:T(8,128)(2,1)S(1)}, bf16[2,16,96,168]{3,2,1,0:T(8,128)(2,1)S(1)}, bf16[2,16,96,168]{3,2,1,0:T(8,128)(2,1)S(1)}, bf16[3,168,...) custom-call(bf16[4,4,96,640]{3,2,1,0:T(8,128)(2,1)S(1)} %all_to_all.27.own_ref, ...), custom_call_target="tpu_custom_call" | custom-call | flops 8000000000 | bytes 4194304 | tf_op jit(solution)/shard_map/turn/pallas_call | solution.py:420
  67.9 0.8 collective-permute-done.other_ref
  68.8 2.3 %middle.1 = (bf16[16,2,96,640]{3,2,1,0:T(8,128)(2,1)S(1)}, bf16[16,256,128]{2,1,0:T(8,128)(2,1)S(1)}, f32[16,128]{1,0:T(8,128)S(1)}, bf16[3,168,384]{2,1,0:T(8,128)(2,1)S(1)}) custom-call(bf16[16,2,96,640]{3,2,1,0:T(8,128)(2,1)S(1)} %get-tuple-element.24.rows_in_ref, ...), custom_call_target="tpu_custom_call", output_to_operand_aliasing={{0}: (0, {})} | custom-call | flops 4000000000 | bytes 4194304 | tf_op jit(solution)/shard_map/middle/pallas_call | solution.py:435
  71.1 2.0 %collective-permute-start.1 = (bf16[16,256,128]{2,1,0:T(8,128)(2,1)S(1)}, bf16[16,256,128]{2,1,0:T(8,128)(2,1)S(1)}, u32[]{:S(2)}, u32[]{:S(2)}) collective-permute-start(bf16[16,256,128]{2,1,0:T(8,128)(2,1)S(1)} %get-tuple-element.34), channel_id=1, source_target_pairs={{0,1},{1,0},{2,3},{3,2},{4,5},{5,4},{6,7},{7,6},{8,9},{9,8},{10,11... | collective-permute-start | bytes 3145736 | tf_op jit(solution)/shard_map/ppermute | solution.py:448
  73.1 2.6 %rest.1 = (f32[16,240,128]{2,1,0:T(8,128)S(1)}, bf16[1,168,3072]{2,1,0:T(8,128)(2,1)}) custom-call(bf16[16,2,96,640]{3,2,1,0:T(8,128)(2,1)S(1)} %get-tuple-element.30.rows_ref, bf16[3,168,384]{2,1,0:T(8,128)(2,1)S(1)} %get-tuple-element.31.hid_ref, bf16[2,16,96,168]{3,2,1,0:T(8,128)(2,1)S(1)} %get-tuple-element.28.gate_t_ref, ...), custom_call_target="tpu_custom_call" | custom-call | flops 4000000000 | bytes 4194304 | tf_op jit(solution)/shard_map/rest/pallas_call | solution.py:449
  75.7 0.0 collective-permute-done.1.got_ref
  75.7 0.2 join.1
  75.9 0.0 copy-start
  75.9 20.5 %all_to_all.28.got_ref = bf16[16,256,128]{2,1,0:T(8,128)(2,1)S(1)} all-to-all(bf16[16,256,128]{2,1,0:T(8,128)(2,1)S(1)} %join.1), channel_id=1, replica_groups={{0,2,4,6,8,10,12,14,16,18,20,22,24,26,28,30},{1,3,5,7,9,11,13,15,17,19,..., dimensions={0} | all-to-all | bytes 2097152 | tf_op jit(solution)/shard_map/all_to_all | solution.py:462
  96.4 0.0 copy-done
  96.5 0.5 fold.1
  96.9 16.2 %all_to_all.29.got_ref = bf16[16,16,128]{2,1,0:T(8,128)(2,1)S(1)} all-to-all(bf16[16,16,128]{2,1,0:T(8,128)(2,1)S(1)} %fold.1), channel_id=1, replica_groups=mesh['expert'=16,'tensor'=32] {'expert'}, dimensions={0} | all-to-all | bytes 131072 | tf_op jit(solution)/shard_map/all_to_all | solution.py:469
  113.1 1.0 combine.1
Async XLA Ops:
  44.4 20.4 %copy-start.1 = (bf16[1,168,3072]{2,1,0:T(8,128)(2,1)S(1)}, bf16[1,168,3072]{2,1,0:T(8,128)(2,1)}, u32[]{:S(2)}) copy-start(bf16[1,168,3072]{2,1,0:T(8,128)(2,1)} %gate_ref.1) | copy-start | bytes 3096580
  44.4 20.4 %copy-start.2 = (bf16[1,168,3072]{2,1,0:T(8,128)(2,1)S(1)}, bf16[1,168,3072]{2,1,0:T(8,128)(2,1)}, u32[]{:S(2)}) copy-start(bf16[1,168,3072]{2,1,0:T(8,128)(2,1)} %up_ref.1) | copy-start | bytes 3096580
  44.4 20.4 %copy-start.3 = (bf16[1,168,3072]{2,1,0:T(8,128)(2,1)S(1)}, bf16[1,168,3072]{2,1,0:T(8,128)(2,1)}, u32[]{:S(2)}) copy-start(bf16[1,168,3072]{2,1,0:T(8,128)(2,1)} %down_ref.1) | copy-start | bytes 3096580
  62.9 5.9 %collective-permute-start = (bf16[4,4,96,640]{3,2,1,0:T(8,128)(2,1)S(1)}, bf16[4,4,96,640]{3,2,1,0:T(8,128)(2,1)S(1)}, u32[]{:S(2)}, u32[]{:S(2)}) collective-permute-start(bf16[4,4,96,640]{3,2,1,0:T(8,128)(2,1)S(1)} %all_to_all.27.own_ref), channel_id=1, source_target_pairs={{0,1},{1,0},{2,3},{3,2},{4,5},{5,4},{6,7},{7,6},{8,9},{9,8},{10,11... | collective-permute-start | bytes 5898248 | tf_op jit(solution)/shard_map/ppermute | solution.py:419
  71.1 4.6 %collective-permute-start.1 = (bf16[16,256,128]{2,1,0:T(8,128)(2,1)S(1)}, bf16[16,256,128]{2,1,0:T(8,128)(2,1)S(1)}, u32[]{:S(2)}, u32[]{:S(2)}) collective-permute-start(bf16[16,256,128]{2,1,0:T(8,128)(2,1)S(1)} %get-tuple-element.34), channel_id=1, source_target_pairs={{0,1},{1,0},{2,3},{3,2},{4,5},{5,4},{6,7},{7,6},{8,9},{9,8},{10,11... | collective-permute-start | bytes 3145736 | tf_op jit(solution)/shard_map/ppermute | solution.py:448
  75.9 20.5 %copy-start = (bf16[6,256,384]{2,1,0:T(8,128)(2,1)S(1)}, bf16[6,256,384]{2,1,0:T(8,128)(2,1)}, u32[]{:S(2)}) copy-start(bf16[6,256,384]{2,1,0:T(8,128)(2,1)} %constant.2.clone.table_ref) | copy-start | bytes 3538948

commit v5 on v4

--- a/solution.py
+++ b/solution.py
@@ -236,13 +236,14 @@
     core = this_core()
     first = core == 0
     for i in range(CHIPS):
-        rows_ref[chip_of(i, core), core] = own_ref[i // SIDE, i % SIDE]
+        rows_ref[chip_of(i, core), core] = own_ref[i // SIDE, i % SIDE, :, 256:640]
     for w, weight_ref in enumerate((gate_ref, up_ref, down_ref)):
+        weight = weight_ref[0]
         for q in range(4):
-            wide = weight_ref[0, :, pl.ds(q * 768, 768)]
-            cut = [wide[:, 96 * p : 96 * p + 96] for p in range(8)]
-            even = jnp.concatenate(cut[0::2], axis=1)
-            odd = jnp.concatenate(cut[1::2], axis=1)
+            even = [192 * (SIDE * q + p) for p in range(4)]
+            odd = [192 * (SIDE * p + q) + 96 for p in range(4)]
+            even = jnp.concatenate([weight[:, c : c + 96] for c in even], axis=1)
+            odd = jnp.concatenate([weight[:, c : c + 96] for c in odd], axis=1)
             near = jnp.where(first, even, odd)
             far = jnp.where(first, odd, even)
             at = pl.ds(q * 384, 384)
@@ -252,7 +253,7 @@
                 turned_ref = (gate_t_ref, up_t_ref)[w]
                 turned_ref[0, pl.ds(q * 4, 4)] = far.T.reshape(4, FEAT, HID)
                 turned_ref[1, pl.ds(q * 4, 4)] = near.T.reshape(4, FEAT, HID)
-    rows = rows_ref[:, core].reshape(D // 2, 640)
+    rows = own_ref[...].reshape(D // 2, 640)
     near_pre_ref[0] = dot(near_ref[0], rows[:, 0:384])
     near_pre_ref[1] = dot(near_ref[1], rows[:, 0:384])
     near_pre_ref[2] = dot(near_ref[2], rows[:, 256:640])
@@ -272,13 +273,9 @@
 
 
 def middle_kernel(
-    rows_in_ref, other_ref, far_ref, near_pre_ref, prob_ref, gate_t_ref, up_t_ref, rows_ref, send_ref, score_ref, hid_ref
+    other_ref, far_ref, near_pre_ref, prob_ref, gate_t_ref, up_t_ref, send_ref, score_ref, hid_ref
 ):
-    del rows_in_ref
-    core = this_core()
-    for i in range(CHIPS):
-        rows_ref[chip_of(i, 1 - core), 1 - core] = other_ref[i // SIDE, i % SIDE]
-    rows = rows_ref[:, 1 - core].reshape(D // 2, 640)
+    rows = other_ref[...].reshape(D // 2, 640)
     x_t = rows[:, 0:384]
     dy_t = rows[:, 256:640]
     pre_gate = near_pre_ref[0] + dot(far_ref[0], x_t)
@@ -307,8 +304,12 @@
     hid_ref[2] = grad_up
 
 
-def rest_kernel(rows_ref, hid_ref, gate_t_ref, up_t_ref, keep_ref, d_down_ref):
-    d_down_ref[0] = dot_last(hid_ref[0], rows_ref[...].reshape(D, 640)[:, 256:640]).astype(BF16)
+def rest_kernel(rows_in_ref, other_ref, hid_ref, gate_t_ref, up_t_ref, keep_ref, d_down_ref, rows_ref):
+    del rows_in_ref
+    core = this_core()
+    for i in range(CHIPS):
+        rows_ref[chip_of(i, 1 - core), 1 - core] = other_ref[i // SIDE, i % SIDE, :, 256:640]
+    d_down_ref[0] = dot_last(hid_ref[0], rows_ref[...].reshape(D, WIDE)).astype(BF16)
     input_grads(1, gate_t_ref, up_t_ref, hid_ref[1], hid_ref[2], keep_ref)
 
 
@@ -317,8 +318,10 @@
     row = iota((16, 128), 0)
     total = score_ref[...] + got + pltpu.roll(got, 13, 0)
     parts = split_rows(jnp.where(row < 3, total, 0.0))
-    for j in range(CHIPS):
-        out_ref[j, 0:240] = (keep_ref[j, 0:240] + got_ref[j, 0:240].astype(F32)).astype(BF16)
+    core = this_core()
+    for i in range(CHIPS):
+        j = chip_of(i, core)
+        out_ref[j, 0:240] = (keep_ref[i, 0:240] + got_ref[i, 0:240].astype(F32)).astype(BF16)
         out_ref[j, 240:256] = parts
 
 
@@ -420,7 +423,7 @@
     rows, gate_t, up_t, far, near_pre, picks = pl.pallas_call(
         turn_kernel,
         out_shape=(
-            struct(CHIPS, 2, FEAT, 640, dtype=BF16),
+            struct(CHIPS, 2, FEAT, WIDE, dtype=BF16),
             struct(2, CHIPS, FEAT, HID, dtype=BF16),
             struct(2, CHIPS, FEAT, HID, dtype=BF16),
             struct(3, HID, D // 2, dtype=BF16),
@@ -432,27 +435,30 @@
         cost_estimate=cost(8e9),
         name="turn",
     )(own, gate_weight, up_weight, down_weight, row_of)
-    rows, send, score, hid = pl.pallas_call(
+    send, score, hid = pl.pallas_call(
         middle_kernel,
         out_shape=(
-            struct(CHIPS, 2, FEAT, 640, dtype=BF16),
             struct(CHIPS, 256, 128, dtype=BF16),
             struct(16, 128, dtype=F32),
             struct(3, HID, WIDE, dtype=BF16),
         ),
-        input_output_aliases={0: 0},
         compiler_params=params(24),
         cost_estimate=cost(4e9),
         name="middle",
-    )(rows, other, far, near_pre, prob_rows, gate_t, up_t)
+    )(other, far, near_pre, prob_rows, gate_t, up_t)
     partner = lax.ppermute(send, "tensor", OTHER_CORE)
-    keep, d_down = pl.pallas_call(
+    keep, d_down, _ = pl.pallas_call(
         rest_kernel,
-        out_shape=(struct(CHIPS, 240, 128, dtype=F32), struct(1, HID, D, dtype=BF16)),
+        out_shape=(
+            struct(CHIPS, 240, 128, dtype=F32),
+            struct(1, HID, D, dtype=BF16),
+            struct(CHIPS, 2, FEAT, WIDE, dtype=BF16),
+        ),
+        input_output_aliases={0: 2},
         compiler_params=params(20),
         cost_estimate=cost(4e9),
         name="rest",
-    )(rows, hid, gate_t, up_t)
+    )(rows, other, hid, gate_t, up_t)
     joined = pl.pallas_call(
         join_kernel,
         out_shape=struct(CHIPS, 256, 128, dtype=BF16),

time: 116 us -> 115 us (level)
  transfers between devices with their start and end apart: 2 -> 2, of which waited for: 1 -> 2; matrix products, arithmetic and copies ran while one was open for 0% -> 0% of each run, Pallas kernels for 5% -> 4%
where the time goes in v5:
time: 115 us; the launch traced here: 114 us
  blocking collectives  96.9 us (84%)
  Pallas kernels  10.7 us (9%)
  starting transfers between devices  3.94 us (3%)
  waiting for transfers between devices  1.57 us (1%)
    all_to_all x1, blocking collectives, per_device(): got = lax.all_to_all(packed, 'expert', 0, 0, tiled=True)  29.7 us
    all_to_all x1, blocking collectives, per_device(): lax.all_to_all(joined, 'tensor', 0, 0, tiled=True, axis_index_groups=SAME...  20.2 us
    all_to_all x1, blocking collectives, per_device(): lax.all_to_all(lines, 'tensor', 0, 0, tiled=True, axis_index_groups=LINES...  18.5 us
    all_to_all x1, blocking collectives, per_device(): back = lax.all_to_all(folded, 'expert', 0, 0, tiled=True)  16.5 us
    all_to_all x1, blocking collectives, per_device(): lax.all_to_all(copies, 'tensor', 0, 0, tiled=True, axis_index_groups=LINE...  12 us
    pallas_call x1, Pallas kernels, per_device(): pl.pallas_call(turn_kernel, out_shape=(struct(CHIPS, 2, FEAT, WIDE, dtype...  2.83 us
  transfers between devices with their start and end apart: 2, of which 2 were waited for; matrix products, arithmetic and copies ran while one was open for 0% of the time, Pallas kernels for 4%

profile of v5, /device:TPU:24, one launch (start us, length us, event | category | flops | bytes accessed | tf_op | source)
XLA Modules:
  0.0 113.8 jit_solution(14941331175297434900)
XLA Ops:
  0.6 1.3 %pack.1 = (bf16[16,32,128]{2,1,0:T(8,128)(2,1)S(1)}, s32[8,64]{1,0:T(8,128)S(1)}) custom-call(s32[4,64]{1,0:T(4,128)} %bitcast.3, bf16[4,64]{1,0:T(4,128)(2,1)} %bitcast.4, bf16[64,96]{1,0:T(8,128)(2,1)} %x_hbm.1, bf16[64,96]{1,0:T(8,128)(2,1)} %dy_hbm.1), custom_call_target="tpu_custom_call" | custom-call | tf_op jit(solution)/shard_map/pack/pallas_call | solution.py:393
  2.0 29.7 %all_to_all.25.got_ref = bf16[16,32,128]{2,1,0:T(8,128)(2,1)S(1)} all-to-all(bf16[16,32,128]{2,1,0:T(8,128)(2,1)S(1)} %get-tuple-element.20), channel_id=1, replica_groups=mesh['expert'=16,'tensor'=32] {'expert'}, dimensions={0} | all-to-all | bytes 262144 | tf_op jit(solution)/shard_map/all_to_all | solution.py:407
  31.7 0.5 spread.1
  32.2 12.0 %all_to_all.26.got_ref = bf16[4,96,640]{2,1,0:T(8,128)(2,1)S(1)} all-to-all(bf16[4,96,640]{2,1,0:T(8,128)(2,1)S(1)} %get-tuple-element.21), channel_id=1, replica_groups={{0,2,4,6},{8,10,12,14},{16,18,20,22},{24,26,28,30},{1,9,17,25},{3,11,19..., dimensions={0} | all-to-all | bytes 983040 | tf_op jit(solution)/shard_map/all_to_all | solution.py:414
  44.2 0.2 relay.1
  44.4 0.0 copy-start.1
  44.4 0.0 copy-start.2
  44.4 0.0 copy-start.3
  44.4 18.5 %all_to_all.27.own_ref = bf16[4,4,96,640]{3,2,1,0:T(8,128)(2,1)S(1)} all-to-all(bf16[4,4,96,640]{3,2,1,0:T(8,128)(2,1)S(1)} %relay.1), channel_id=1, replica_groups={{0,8,16,24},{2,10,18,26},{4,12,20,28},{6,14,22,30},{1,3,5,7},{9,11,13,1..., dimensions={0} | all-to-all | bytes 3932160 | tf_op jit(solution)/shard_map/all_to_all | solution.py:421
  62.9 1.9 %collective-permute-start = (bf16[4,4,96,640]{3,2,1,0:T(8,128)(2,1)S(1)}, bf16[4,4,96,640]{3,2,1,0:T(8,128)(2,1)S(1)}, u32[]{:S(2)}, u32[]{:S(2)}) collective-permute-start(bf16[4,4,96,640]{3,2,1,0:T(8,128)(2,1)S(1)} %all_to_all.27.own_ref), channel_id=1, source_target_pairs={{0,1},{1,0},{2,3},{3,2},{4,5},{5,4},{6,7},{7,6},{8,9},{9,8},{10,11... | collective-permute-start | bytes 5898248 | tf_op jit(solution)/shard_map/ppermute | solution.py:422
  64.8 0.0 copy-done.1
  64.8 0.0 copy-done.2
  64.8 0.0 copy-done.3
  64.8 2.8 %turn.1 = (bf16[16,2,96,384]{3,2,1,0:T(8,128)(2,1)S(1)}, bf16[2,16,96,168]{3,2,1,0:T(8,128)(2,1)S(1)}, bf16[2,16,96,168]{3,2,1,0:T(8,128)(2,1)S(1)}, bf16[3,168,...) custom-call(bf16[4,4,96,640]{3,2,1,0:T(8,128)(2,1)S(1)} %all_to_all.27.own_ref, ...), custom_call_target="tpu_custom_call" | custom-call | flops 8000000000 | bytes 4194304 | tf_op jit(solution)/shard_map/turn/pallas_call | solution.py:423
  67.7 1.1 collective-permute-done.other_ref
  68.8 2.1 %middle.1 = (bf16[16,256,128]{2,1,0:T(8,128)(2,1)S(1)}, f32[16,128]{1,0:T(8,128)S(1)}, bf16[3,168,384]{2,1,0:T(8,128)(2,1)S(1)}) custom-call(bf16[4,4,96,640]{3,2,1,0:T(8,128)(2,1)S(1)} %collective-permute-done.other_ref, bf16[3,168,1536]{2,1,0:T(8,128)(2,1)S(1)} %get-tuple-element.24.far_ref, f32[3,168,384]{2,1,0:T(8,128)S(1)} %get-tuple-element.25.near_pre_ref, ...), custom_call_target="tpu_custom_call" | custom-call | flops 4000000000 | bytes 4194304 | tf_op jit(solution)/shard_map/middle/pallas_call | solution.py:438
  70.9 2.0 %collective-permute-start.1 = (bf16[16,256,128]{2,1,0:T(8,128)(2,1)S(1)}, bf16[16,256,128]{2,1,0:T(8,128)(2,1)S(1)}, u32[]{:S(2)}, u32[]{:S(2)}) collective-permute-start(bf16[16,256,128]{2,1,0:T(8,128)(2,1)S(1)} %get-tuple-element.32), channel_id=1, source_target_pairs={{0,1},{1,0},{2,3},{3,2},{4,5},{5,4},{6,7},{7,6},{8,9},{9,8},{10,11... | collective-permute-start | bytes 3145736 | tf_op jit(solution)/shard_map/ppermute | solution.py:449
  72.9 2.0 %rest.1 = (f32[16,240,128]{2,1,0:T(8,128)S(1)}, bf16[1,168,3072]{2,1,0:T(8,128)(2,1)}, bf16[16,2,96,384]{3,2,1,0:T(8,128)(2,1)S(1)}) custom-call(bf16[16,2,96,384]{3,2,1,0:T(8,128)(2,1)S(1)} %get-tuple-element.23.rows_in_ref, bf16[4,4,96,640]{3,2,1,0:T(8,128)(2,1)S(1)} %collective-permute-done.other_ref, ...), custom_call_target="tpu_custom_call", output_to_operand_aliasing={{2}: (0, {})} | custom-call | flops 4000000000 | bytes 4194304 | tf_op jit(solution)/shard_map/rest/pallas_call | solution.py:450
  74.9 0.5 collective-permute-done.1.got_ref
  75.4 0.2 join.1
  75.6 0.0 copy-start
  75.6 20.2 %all_to_all.28.got_ref = bf16[16,256,128]{2,1,0:T(8,128)(2,1)S(1)} all-to-all(bf16[16,256,128]{2,1,0:T(8,128)(2,1)S(1)} %join.1), channel_id=1, replica_groups={{0,2,4,6,8,10,12,14,16,18,20,22,24,26,28,30},{1,3,5,7,9,11,13,15,17,19,..., dimensions={0} | all-to-all | bytes 2097152 | tf_op jit(solution)/shard_map/all_to_all | solution.py:468
  95.8 0.0 copy-done
  95.8 0.5 fold.1
  96.3 16.5 %all_to_all.29.got_ref = bf16[16,16,128]{2,1,0:T(8,128)(2,1)S(1)} all-to-all(bf16[16,16,128]{2,1,0:T(8,128)(2,1)S(1)} %fold.1), channel_id=1, replica_groups=mesh['expert'=16,'tensor'=32] {'expert'}, dimensions={0} | all-to-all | bytes 131072 | tf_op jit(solution)/shard_map/all_to_all | solution.py:475
  112.8 1.0 combine.1
Async XLA Ops:
  44.4 20.4 %copy-start.1 = (bf16[1,168,3072]{2,1,0:T(8,128)(2,1)S(1)}, bf16[1,168,3072]{2,1,0:T(8,128)(2,1)}, u32[]{:S(2)}) copy-start(bf16[1,168,3072]{2,1,0:T(8,128)(2,1)} %gate_ref.1) | copy-start | bytes 3096580
  44.4 20.4 %copy-start.2 = (bf16[1,168,3072]{2,1,0:T(8,128)(2,1)S(1)}, bf16[1,168,3072]{2,1,0:T(8,128)(2,1)}, u32[]{:S(2)}) copy-start(bf16[1,168,3072]{2,1,0:T(8,128)(2,1)} %up_ref.1) | copy-start | bytes 3096580
  44.4 20.4 %copy-start.3 = (bf16[1,168,3072]{2,1,0:T(8,128)(2,1)S(1)}, bf16[1,168,3072]{2,1,0:T(8,128)(2,1)}, u32[]{:S(2)}) copy-start(bf16[1,168,3072]{2,1,0:T(8,128)(2,1)} %down_ref.1) | copy-start | bytes 3096580
  62.9 5.9 %collective-permute-start = (bf16[4,4,96,640]{3,2,1,0:T(8,128)(2,1)S(1)}, bf16[4,4,96,640]{3,2,1,0:T(8,128)(2,1)S(1)}, u32[]{:S(2)}, u32[]{:S(2)}) collective-permute-start(bf16[4,4,96,640]{3,2,1,0:T(8,128)(2,1)S(1)} %all_to_all.27.own_ref), channel_id=1, source_target_pairs={{0,1},{1,0},{2,3},{3,2},{4,5},{5,4},{6,7},{7,6},{8,9},{9,8},{10,11... | collective-permute-start | bytes 5898248 | tf_op jit(solution)/shard_map/ppermute | solution.py:422
  70.9 4.5 %collective-permute-start.1 = (bf16[16,256,128]{2,1,0:T(8,128)(2,1)S(1)}, bf16[16,256,128]{2,1,0:T(8,128)(2,1)S(1)}, u32[]{:S(2)}, u32[]{:S(2)}) collective-permute-start(bf16[16,256,128]{2,1,0:T(8,128)(2,1)S(1)} %get-tuple-element.32), channel_id=1, source_target_pairs={{0,1},{1,0},{2,3},{3,2},{4,5},{5,4},{6,7},{7,6},{8,9},{9,8},{10,11... | collective-permute-start | bytes 3145736 | tf_op jit(solution)/shard_map/ppermute | solution.py:449
  75.6 20.2 %copy-start = (bf16[6,256,384]{2,1,0:T(8,128)(2,1)S(1)}, bf16[6,256,384]{2,1,0:T(8,128)(2,1)}, u32[]{:S(2)}) copy-start(bf16[6,256,384]{2,1,0:T(8,128)(2,1)} %constant.2.clone.table_ref) | copy-start | bytes 3538948

commit v6 on v5

--- a/solution.py
+++ b/solution.py
@@ -289,7 +289,6 @@
     silu = pre_gate * sig
     hidden = (silu * pre_up).astype(BF16).astype(F32)
     scores = score_rows(jnp.sum(hidden * back, axis=0, keepdims=True))
-    scaled = jnp.where(live, probs * hidden, 0.0)
     back_p = probs * back
     grad_gate = jnp.where(live, back_p * pre_up * sig * (1.0 + pre_gate * (1.0 - sig)), 0.0).astype(BF16)
     grad_up = (back_p * silu).astype(BF16)
@@ -298,18 +297,22 @@
     for j in range(CHIPS):
         send_ref[j, 240:256] = parts
     score_ref[...] = scores
-    scaled = jnp.concatenate([pltpu.roll(scaled[:, 256:384], 64, 1), scaled[:, 0:256]], axis=1)
-    hid_ref[0] = scaled.astype(BF16)
+    hid_ref[0] = hidden.astype(BF16)
     hid_ref[1] = grad_gate
     hid_ref[2] = grad_up
 
 
-def rest_kernel(rows_in_ref, other_ref, hid_ref, gate_t_ref, up_t_ref, keep_ref, d_down_ref, rows_ref):
+def rest_kernel(
+    rows_in_ref, other_ref, hid_ref, prob_ref, gate_t_ref, up_t_ref, keep_ref, d_down_ref, rows_ref
+):
     del rows_in_ref
     core = this_core()
     for i in range(CHIPS):
         rows_ref[chip_of(i, 1 - core), 1 - core] = other_ref[i // SIDE, i % SIDE, :, 256:640]
-    d_down_ref[0] = dot_last(hid_ref[0], rows_ref[...].reshape(D, WIDE)).astype(BF16)
+    live = iota((1, WIDE), 1) < SLOTS
+    scaled = jnp.where(live, prob_ref[0:1, :] * hid_ref[0].astype(F32), 0.0)
+    scaled = jnp.concatenate([pltpu.roll(scaled[:, 256:384], 64, 1), scaled[:, 0:256]], axis=1).astype(BF16)
+    d_down_ref[0] = dot_last(scaled, rows_ref[...].reshape(D, WIDE)).astype(BF16)
     input_grads(1, gate_t_ref, up_t_ref, hid_ref[1], hid_ref[2], keep_ref)
 
 
@@ -458,7 +461,7 @@
         compiler_params=params(20),
         cost_estimate=cost(4e9),
         name="rest",
-    )(rows, other, hid, gate_t, up_t)
+    )(rows, other, hid, prob_rows, gate_t, up_t)
     joined = pl.pallas_call(
         join_kernel,
         out_shape=struct(CHIPS, 256, 128, dtype=BF16),

time: 115 us -> 116 us (level)
  transfers between devices with their start and end apart: 2 -> 2, of which waited for: 2 -> 1; matrix products, arithmetic and copies ran while one was open for 0% -> 0% of each run, Pallas kernels for 4% -> 5%
where the time goes in v6:
time: 116 us; the launch traced here: 114 us
  blocking collectives  96.9 us (84%)
  Pallas kernels  11.4 us (10%)
  starting transfers between devices  3.94 us (3%)
    all_to_all x1, blocking collectives, per_device(): got = lax.all_to_all(packed, 'expert', 0, 0, tiled=True)  29.7 us
    all_to_all x1, blocking collectives, per_device(): lax.all_to_all(joined, 'tensor', 0, 0, tiled=True, axis_index_groups=SAME...  20.5 us
    all_to_all x1, blocking collectives, per_device(): lax.all_to_all(lines, 'tensor', 0, 0, tiled=True, axis_index_groups=LINES...  18.5 us
    all_to_all x1, blocking collectives, per_device(): back = lax.all_to_all(folded, 'expert', 0, 0, tiled=True)  16.2 us
    all_to_all x1, blocking collectives, per_device(): lax.all_to_all(copies, 'tensor', 0, 0, tiled=True, axis_index_groups=LINE...  12 us
    pallas_call x1, Pallas kernels, per_device(): pl.pallas_call(turn_kernel, out_shape=(struct(CHIPS, 2, FEAT, WIDE, dtype...  2.83 us
    pallas_call x1, Pallas kernels, per_device(): pl.pallas_call(rest_kernel, out_shape=(struct(CHIPS, 240, 128, dtype=F32)...  2.71 us
  transfers between devices with their start and end apart: 2, of which 1 were waited for; matrix products, arithmetic and copies ran while one was open for 0% of the time, Pallas kernels for 5%

profile of v6, /device:TPU:24, one launch (start us, length us, event | category | flops | bytes accessed | tf_op | source)
XLA Modules:
  0.0 114.0 jit_solution(854653386531581667)
XLA Ops:
  0.6 1.3 %pack.1 = (bf16[16,32,128]{2,1,0:T(8,128)(2,1)S(1)}, s32[8,64]{1,0:T(8,128)S(1)}) custom-call(s32[4,64]{1,0:T(4,128)} %bitcast.3, bf16[4,64]{1,0:T(4,128)(2,1)} %bitcast.4, bf16[64,96]{1,0:T(8,128)(2,1)} %x_hbm.1, bf16[64,96]{1,0:T(8,128)(2,1)} %dy_hbm.1), custom_call_target="tpu_custom_call" | custom-call | tf_op jit(solution)/shard_map/pack/pallas_call | solution.py:396
  2.0 29.7 %all_to_all.25.got_ref = bf16[16,32,128]{2,1,0:T(8,128)(2,1)S(1)} all-to-all(bf16[16,32,128]{2,1,0:T(8,128)(2,1)S(1)} %get-tuple-element.20), channel_id=1, replica_groups=mesh['expert'=16,'tensor'=32] {'expert'}, dimensions={0} | all-to-all | bytes 262144 | tf_op jit(solution)/shard_map/all_to_all | solution.py:410
  31.7 0.5 spread.1
  32.2 12.0 %all_to_all.26.got_ref = bf16[4,96,640]{2,1,0:T(8,128)(2,1)S(1)} all-to-all(bf16[4,96,640]{2,1,0:T(8,128)(2,1)S(1)} %get-tuple-element.21), channel_id=1, replica_groups={{0,2,4,6},{8,10,12,14},{16,18,20,22},{24,26,28,30},{1,9,17,25},{3,11,19..., dimensions={0} | all-to-all | bytes 983040 | tf_op jit(solution)/shard_map/all_to_all | solution.py:417
  44.2 0.2 relay.1
  44.4 0.0 copy-start.1
  44.4 0.0 copy-start.2
  44.4 0.0 copy-start.3
  44.4 18.5 %all_to_all.27.own_ref = bf16[4,4,96,640]{3,2,1,0:T(8,128)(2,1)S(1)} all-to-all(bf16[4,4,96,640]{3,2,1,0:T(8,128)(2,1)S(1)} %relay.1), channel_id=1, replica_groups={{0,8,16,24},{2,10,18,26},{4,12,20,28},{6,14,22,30},{1,3,5,7},{9,11,13,1..., dimensions={0} | all-to-all | bytes 3932160 | tf_op jit(solution)/shard_map/all_to_all | solution.py:424
  62.9 1.9 %collective-permute-start = (bf16[4,4,96,640]{3,2,1,0:T(8,128)(2,1)S(1)}, bf16[4,4,96,640]{3,2,1,0:T(8,128)(2,1)S(1)}, u32[]{:S(2)}, u32[]{:S(2)}) collective-permute-start(bf16[4,4,96,640]{3,2,1,0:T(8,128)(2,1)S(1)} %all_to_all.27.own_ref), channel_id=1, source_target_pairs={{0,1},{1,0},{2,3},{3,2},{4,5},{5,4},{6,7},{7,6},{8,9},{9,8},{10,11... | collective-permute-start | bytes 5898248 | tf_op jit(solution)/shard_map/ppermute | solution.py:425
  64.8 0.0 copy-done.1
  64.8 0.0 copy-done.2
  64.8 0.0 copy-done.3
  64.8 2.8 %turn.1 = (bf16[16,2,96,384]{3,2,1,0:T(8,128)(2,1)S(1)}, bf16[2,16,96,168]{3,2,1,0:T(8,128)(2,1)S(1)}, bf16[2,16,96,168]{3,2,1,0:T(8,128)(2,1)S(1)}, bf16[3,168,...) custom-call(bf16[4,4,96,640]{3,2,1,0:T(8,128)(2,1)S(1)} %all_to_all.27.own_ref, ...), custom_call_target="tpu_custom_call" | custom-call | flops 8000000000 | bytes 4194304 | tf_op jit(solution)/shard_map/turn/pallas_call | solution.py:426
  67.7 1.1 collective-permute-done.other_ref
  68.8 2.1 %middle.1 = (bf16[16,256,128]{2,1,0:T(8,128)(2,1)S(1)}, f32[16,128]{1,0:T(8,128)S(1)}, bf16[3,168,384]{2,1,0:T(8,128)(2,1)S(1)}) custom-call(bf16[4,4,96,640]{3,2,1,0:T(8,128)(2,1)S(1)} %collective-permute-done.other_ref, bf16[3,168,1536]{2,1,0:T(8,128)(2,1)S(1)} %get-tuple-element.24.far_ref, f32[3,168,384]{2,1,0:T(8,128)S(1)} %get-tuple-element.25.near_pre_ref, ...), custom_call_target="tpu_custom_call" | custom-call | flops 4000000000 | bytes 4194304 | tf_op jit(solution)/shard_map/middle/pallas_call | solution.py:441
  70.9 2.0 %collective-permute-start.1 = (bf16[16,256,128]{2,1,0:T(8,128)(2,1)S(1)}, bf16[16,256,128]{2,1,0:T(8,128)(2,1)S(1)}, u32[]{:S(2)}, u32[]{:S(2)}) collective-permute-start(bf16[16,256,128]{2,1,0:T(8,128)(2,1)S(1)} %get-tuple-element.32), channel_id=1, source_target_pairs={{0,1},{1,0},{2,3},{3,2},{4,5},{5,4},{6,7},{7,6},{8,9},{9,8},{10,11... | collective-permute-start | bytes 3145736 | tf_op jit(solution)/shard_map/ppermute | solution.py:452
  72.9 2.7 %rest.1 = (f32[16,240,128]{2,1,0:T(8,128)S(1)}, bf16[1,168,3072]{2,1,0:T(8,128)(2,1)}, bf16[16,2,96,384]{3,2,1,0:T(8,128)(2,1)S(1)}) custom-call(bf16[16,2,96,384]{3,2,1,0:T(8,128)(2,1)S(1)} %get-tuple-element.23.rows_in_ref, bf16[4,4,96,640]{3,2,1,0:T(8,128)(2,1)S(1)} %collective-permute-done.other_ref, ...), custom_call_target="tpu_custom_call", output_to_operand_aliasing={{2}: (0, {})} | custom-call | flops 4000000000 | bytes 4194304 | tf_op jit(solution)/shard_map/rest/pallas_call | solution.py:453
  75.6 0.0 collective-permute-done.1.got_ref
  75.6 0.2 join.1
  75.8 0.0 copy-start
  75.8 20.5 %all_to_all.28.got_ref = bf16[16,256,128]{2,1,0:T(8,128)(2,1)S(1)} all-to-all(bf16[16,256,128]{2,1,0:T(8,128)(2,1)S(1)} %join.1), channel_id=1, replica_groups={{0,2,4,6,8,10,12,14,16,18,20,22,24,26,28,30},{1,3,5,7,9,11,13,15,17,19,..., dimensions={0} | all-to-all | bytes 2097152 | tf_op jit(solution)/shard_map/all_to_all | solution.py:471
  96.3 0.0 copy-done
  96.3 0.5 fold.1
  96.8 16.2 %all_to_all.29.got_ref = bf16[16,16,128]{2,1,0:T(8,128)(2,1)S(1)} all-to-all(bf16[16,16,128]{2,1,0:T(8,128)(2,1)S(1)} %fold.1), channel_id=1, replica_groups=mesh['expert'=16,'tensor'=32] {'expert'}, dimensions={0} | all-to-all | bytes 131072 | tf_op jit(solution)/shard_map/all_to_all | solution.py:478
  113.0 1.0 combine.1
Async XLA Ops:
  44.4 20.4 %copy-start.1 = (bf16[1,168,3072]{2,1,0:T(8,128)(2,1)S(1)}, bf16[1,168,3072]{2,1,0:T(8,128)(2,1)}, u32[]{:S(2)}) copy-start(bf16[1,168,3072]{2,1,0:T(8,128)(2,1)} %gate_ref.1) | copy-start | bytes 3096580
  44.4 20.4 %copy-start.2 = (bf16[1,168,3072]{2,1,0:T(8,128)(2,1)S(1)}, bf16[1,168,3072]{2,1,0:T(8,128)(2,1)}, u32[]{:S(2)}) copy-start(bf16[1,168,3072]{2,1,0:T(8,128)(2,1)} %up_ref.1) | copy-start | bytes 3096580
  44.4 20.4 %copy-start.3 = (bf16[1,168,3072]{2,1,0:T(8,128)(2,1)S(1)}, bf16[1,168,3072]{2,1,0:T(8,128)(2,1)}, u32[]{:S(2)}) copy-start(bf16[1,168,3072]{2,1,0:T(8,128)(2,1)} %down_ref.1) | copy-start | bytes 3096580
  62.9 5.9 %collective-permute-start = (bf16[4,4,96,640]{3,2,1,0:T(8,128)(2,1)S(1)}, bf16[4,4,96,640]{3,2,1,0:T(8,128)(2,1)S(1)}, u32[]{:S(2)}, u32[]{:S(2)}) collective-permute-start(bf16[4,4,96,640]{3,2,1,0:T(8,128)(2,1)S(1)} %all_to_all.27.own_ref), channel_id=1, source_target_pairs={{0,1},{1,0},{2,3},{3,2},{4,5},{5,4},{6,7},{7,6},{8,9},{9,8},{10,11... | collective-permute-start | bytes 5898248 | tf_op jit(solution)/shard_map/ppermute | solution.py:425
  70.9 4.8 %collective-permute-start.1 = (bf16[16,256,128]{2,1,0:T(8,128)(2,1)S(1)}, bf16[16,256,128]{2,1,0:T(8,128)(2,1)S(1)}, u32[]{:S(2)}, u32[]{:S(2)}) collective-permute-start(bf16[16,256,128]{2,1,0:T(8,128)(2,1)S(1)} %get-tuple-element.32), channel_id=1, source_target_pairs={{0,1},{1,0},{2,3},{3,2},{4,5},{5,4},{6,7},{7,6},{8,9},{9,8},{10,11... | collective-permute-start | bytes 3145736 | tf_op jit(solution)/shard_map/ppermute | solution.py:452
  75.8 20.5 %copy-start = (bf16[6,256,384]{2,1,0:T(8,128)(2,1)S(1)}, bf16[6,256,384]{2,1,0:T(8,128)(2,1)}, u32[]{:S(2)}) copy-start(bf16[6,256,384]{2,1,0:T(8,128)(2,1)} %constant.2.clone.table_ref) | copy-start | bytes 3538948
